TPU v7x, 32 devices: a whole 2x2x4 slice. The times are simulated.
32 devices in a mesh: dom: 4 (over z), cls: 8 (over y, x, core).
Axes of the slice: x: 2, y: 2, z: 4, core: 2. Of those that a mesh axis runs over, the one named last changes fastest.
Arguments:
- images: bfloat16 [1024, 64, 256], P(('dom', 'cls'))
- references: bfloat16 [128, 64, 256], P('cls')
- ctf_table: float32 [64, 64], replicated, may hold values from 0.2 to 1
- defocus: int32 [1024], P(('dom', 'cls')), may hold values from 0 to 63
- priors: int32 [1024, 8], P(('dom', 'cls')), may hold values from 0 to 127, as said below
Outputs:
- new_refs: float32 [128, 64, 256], P('cls', 'dom')
Inputs may be any that keep to these rules, and one draw needn't show every extreme that they name: `priors`: the owner of class k is index k // 16 of cls. Among the prior entries of one device's particles at most 40 name classes of any one owner; in each index of dom one owner is named exactly 40 times by every device.
All inputs are finite; a program needn't handle non-finite values.
Results may differ from a plain program's by a relative error of at most 0.011.
Values may be sent and summed in bfloat16 or wider, within the bound.
A program may use at most 128 MiB of HBM per device.

v0:
```python
import math

import jax
import jax.numpy as jnp
from jax import lax
from jax.sharding import PartitionSpec as P


def angle_tables(angles):
    harm_count = angles // 2
    angle_index = jnp.arange(angles, dtype=jnp.int32)
    harm_index = jnp.arange(harm_count, dtype=jnp.int32)
    phase_grid = angle_index[:, None] * harm_index[None, :] % angles
    angle_grid = 2.0 * jnp.pi / angles * phase_grid.astype(jnp.float32)
    cosine = jnp.cos(angle_grid)
    sine_grid = jnp.sin(angle_grid)
    forward = jnp.concatenate([cosine, sine_grid], axis=1)
    harm_weight = jnp.where(harm_index == 0, 1.0, 2.0).astype(jnp.float32) / angles
    inverse = jnp.concatenate(
        [cosine.T * harm_weight[:, None], -sine_grid.T * harm_weight[:, None]], axis=0
    )
    return (forward, inverse)


def to_harmonics(frames, forward):
    frame_count, cycle_count, angles = frames.shape
    flat_rows = jnp.dot(
        frames.reshape(frame_count * cycle_count, angles),
        forward.astype(jnp.bfloat16),
        preferred_element_type=jnp.float32,
    )
    return flat_rows.astype(jnp.bfloat16).reshape(frame_count, cycle_count, forward.shape[1])


def slot_scores(part_block, ref_block, ctf_block, inverse):
    harm_count = part_block.shape[2] // 2
    part_cos = part_block[:, :, :harm_count].astype(jnp.float32)
    part_sin = part_block[:, :, harm_count:].astype(jnp.float32)
    ref_cos = ref_block[:, :, :harm_count].astype(jnp.float32)
    ref_sin = ref_block[:, :, harm_count:].astype(jnp.float32)
    ctf_weight = ctf_block[:, :, None]
    real_part = jnp.sum(ctf_weight * (part_cos * ref_cos + part_sin * ref_sin), axis=1)
    imag_part = jnp.sum(ctf_weight * (part_cos * ref_sin - part_sin * ref_cos), axis=1)
    joined = jnp.concatenate([real_part, imag_part], axis=1)
    return jnp.dot(joined, inverse, precision=lax.Precision.HIGHEST)


def accumulate_terms(part_block, weights, ctf_block, forward):
    harm_count = part_block.shape[2] // 2
    spectrum = jnp.dot(weights, forward, precision=lax.Precision.HIGHEST)
    w_cos = spectrum[:, None, :harm_count]
    w_sin = spectrum[:, None, harm_count:]
    part_cos = part_block[:, :, :harm_count].astype(jnp.float32)
    part_sin = part_block[:, :, harm_count:].astype(jnp.float32)
    ctf_weight = ctf_block[:, :, None]
    real_part = ctf_weight * (part_cos * w_cos + part_sin * w_sin)
    imag_part = ctf_weight * (part_sin * w_cos - part_cos * w_sin)
    term_rows = jnp.concatenate([real_part, imag_part], axis=2)
    norm_rows = ctf_block * ctf_block * jnp.sum(weights, axis=1)[:, None]
    return (term_rows, norm_rows)


def on_device(images, references, ctf_table, defocus, priors):
    owners = lax.axis_size("cls")
    owned = references.shape[0]
    particles = images.shape[0]
    cycle_count = images.shape[1]
    angles = images.shape[2]
    prior_count = priors.shape[1]
    capacity = 5 * particles * prior_count // (4 * owners)
    send_rows = owners * capacity
    forward, inverse = angle_tables(angles)
    classes = priors.reshape(-1)
    target = classes // owned
    local_class = classes - target * owned
    owner_hits = (target[:, None] == jnp.arange(owners, dtype=jnp.int32)[None, :]).astype(jnp.int32)
    earlier = jnp.cumsum(owner_hits, axis=0) - owner_hits
    places = target * capacity + jnp.sum(earlier * owner_hits, axis=1)
    source = jnp.arange(particles * prior_count, dtype=jnp.int32) // prior_count
    class_buffer = jnp.full((send_rows,), -1, jnp.int32).at[places].set(local_class)
    group_buffer = jnp.zeros((send_rows,), jnp.int32).at[places].set(defocus[source])
    harmonic = to_harmonics(images, forward)
    payload = (
        jnp.zeros((send_rows, cycle_count, harmonic.shape[2]), jnp.bfloat16)
        .at[places]
        .set(harmonic[source])
    )
    received, got_class, got_group = (
        lax.all_to_all(payload, "cls", split_axis=0, concat_axis=0, tiled=True),
        lax.all_to_all(class_buffer, "cls", split_axis=0, concat_axis=0, tiled=True),
        lax.all_to_all(group_buffer, "cls", split_axis=0, concat_axis=0, tiled=True),
    )
    ref_harm = to_harmonics(references, forward)
    group_total = ctf_table.shape[0]
    group_hits = (got_group[:, None] == jnp.arange(group_total, dtype=jnp.int32)[None, :]).astype(
        jnp.float32
    )
    ctf_rows = jnp.dot(group_hits, ctf_table, precision=lax.Precision.HIGHEST)
    filled = got_class >= 0
    class_index = jnp.maximum(got_class, 0)
    block_rows = math.gcd(64, send_rows)
    block_count = send_rows // block_rows
    part_blocks = received.reshape(block_count, block_rows, cycle_count, received.shape[2])
    pick_blocks = class_index.reshape(block_count, block_rows)
    ctf_blocks = ctf_rows.reshape(block_count, block_rows, cycle_count)

    def score_block(inputs):
        part_block, pick_block, ctf_block = inputs
        return slot_scores(part_block, jnp.take(ref_harm, pick_block, axis=0), ctf_block, inverse)

    scores = lax.map(score_block, (part_blocks, pick_blocks, ctf_blocks)).reshape(send_rows, angles)
    returned = lax.all_to_all(scores, "cls", split_axis=0, concat_axis=0, tiled=True)
    grouped = returned[places].reshape(particles, prior_count * angles)
    highest = jnp.max(grouped, axis=1, keepdims=True)
    log_total = highest + jnp.log(jnp.sum(jnp.exp(grouped - highest), axis=1, keepdims=True))
    normal_buffer = (
        jnp.zeros((send_rows,), jnp.float32)
        .at[places]
        .set(jnp.repeat(log_total.reshape(-1), prior_count))
    )
    got_log = lax.all_to_all(normal_buffer, "cls", split_axis=0, concat_axis=0, tiled=True)
    weights = jnp.where(filled[:, None], jnp.exp(scores - got_log[:, None]), 0.0)
    weight_blocks = weights.reshape(block_count, block_rows, angles)
    live_blocks = filled.reshape(block_count, block_rows)
    class_range = jnp.arange(owned, dtype=jnp.int32)

    def add_block(carry, inputs):
        class_sums, class_norms = carry
        part_block, pick_block, ctf_block, block_weights, live_block = inputs
        term_rows, norm_rows = accumulate_terms(part_block, block_weights, ctf_block, forward)
        member = ((pick_block[:, None] == class_range[None, :]) & live_block[:, None]).astype(
            jnp.float32
        )
        class_sums = class_sums + jnp.dot(
            member.T, term_rows.reshape(block_rows, -1), precision=lax.Precision.HIGHEST
        )
        class_norms = class_norms + jnp.dot(member.T, norm_rows, precision=lax.Precision.HIGHEST)
        return ((class_sums, class_norms), None)

    initial = (
        jnp.zeros((owned, cycle_count * received.shape[2]), jnp.float32),
        jnp.zeros((owned, cycle_count), jnp.float32),
    )
    (class_sums, class_norms), ignored = lax.scan(
        add_block, initial, (part_blocks, pick_blocks, ctf_blocks, weight_blocks, live_blocks)
    )
    part_sums, part_norms = (
        lax.psum_scatter(
            class_sums.reshape(owned, cycle_count, received.shape[2]),
            "dom",
            scatter_dimension=1,
            tiled=True,
        ),
        lax.psum_scatter(class_norms, "dom", scatter_dimension=1, tiled=True),
    )
    return part_sums / (part_norms + 1.0)[:, :, None]


def solution(mesh):
    return jax.shard_map(
        on_device,
        mesh=mesh,
        in_specs=(
            P(("dom", "cls"), None, None),
            P("cls", None, None),
            P(),
            P(("dom", "cls")),
            P(("dom", "cls"), None),
        ),
        out_specs=P("cls", "dom", None),
        check_vma=False,
    )
```

profile of v0, /device:TPU:0, one launch (start us, length us, event | category | flops | bytes accessed | tf_op | source)
XLA Modules:
  0.0 406.2 jit_solution(14846766194699724121)
XLA Ops:
  6.5 2.1 fusion.64
  8.6 1.8 fusion.65
  12.5 20.1 %compare_select_fusion.7 = s32[256]{0:T(256)S(1)} fusion(s32[256]{0:T(256)S(1)} %bitcast.160, s32[]{:T(128)} %bitcast.11, s32[]{:T(128)} %bitcast.12, s32[]{:T(128)} %bitcast.13, s32[]{:T(128)} %bitcast.14, s32[]{:T(128)} %bitcast.15, s32[]{:T(128)} %bitcast.16, s32[]{:T(128)} %bitcast.17, s32[]{:T(128)} %bitcast.18, s32[]{:T(128)} %bitcast.19, ...), kind=kLoop, calls=%fused_computation.121 | loop fusion | flops 15872 | bytes 2176 | tf_op jit(solution)/shard_map/gather | solution.py:81
  34.6 5.2 %all-to-all-start.1 = ((s32[8,40,1]{1,2,0:T(1,128)}), s32[8,40,1]{1,2,0:T(1,128)S(1)}, u32[]{:S(2)}, u32[]{:S(2)}) async-start(s32[8,40,1]{1,2,0:T(1,128)} %bitcast.43), calls=%async_computation.1 | async-start | bytes 8192 | tf_op jit(solution)/shard_map/all_to_all | solution.py:91
  44.4 3.2 all-to-all-start
  48.2 8.6 %gather_fusion.1 = bf16[256,64,256]{2,1,0:T(8,128)(2,1)} fusion(bf16[32,64,256]{2,1,0:T(8,128)(2,1)S(1)} %bitcast.147, s32[1024]{0:T(1024)S(1)} %pad_clamp_fusion.2), kind=kCustom, calls=%fused_computation.1 | custom fusion | bytes 16778240 | tf_op jit(solution)/shard_map/gather | solution.py:86
  56.8 5.2 %broadcast_in_dim.50 = bf16[320,64,256]{2,1,0:T(8,128)(2,1)} broadcast(bf16[]{:T(256)} %constant.108.clone.1), dimensions={} | broadcast | bytes 10485762 | tf_op jit(solution)/shard_map/broadcast_in_dim | solution.py:84
  62.0 37.3 %scatter_fusion = bf16[320,64,256]{2,1,0:T(8,128)(2,1)} fusion(bf16[320,64,256]{2,1,0:T(8,128)(2,1)} %broadcast_in_dim.50, s32[256]{0:T(256)S(1)} %bitcast.156, bf16[256,64,256]{2,1,0:T(8,128)(2,1)} %gather_fusion.1), kind=kCustom, calls=%fused_computation.5 | custom fusion | bytes 25166848 | tf_op jit(solution)/shard_map/scatter | solution.py:86
  99.3 5.3 %all-to-all-start.2 = ((bf16[320,64,256]{2,1,0:T(8,128)(2,1)}), bf16[320,64,256]{2,1,0:T(8,128)(2,1)}, u32[]{:S(2)}, u32[]{:S(2)}) async-start(bf16[320,64,256]{2,1,0:T(8,128)(2,1)} %scatter_fusion), calls=%async_computation.2 | async-start | bytes 20971520 | tf_op jit(solution)/shard_map/all_to_all | solution.py:89
  107.4 113.7 %all-to-all-done.2 = bf16[320,64,256]{2,1,0:T(8,128)(2,1)} async-done(((bf16[320,64,256]{2,1,0:T(8,128)(2,1)}), bf16[320,64,256]{2,1,0:T(8,128)(2,1)}, u32[]{:S(2)}, u32[]{:S(2)}) %all-to-all-start.2) | async-done | bytes 10485792 | tf_op jit(solution)/shard_map/all_to_all | solution.py:89
  221.1 39.0 %while.25 = (s32[]{:T(128)}, f32[5,64,256]{2,1,0:T(8,128)}, f32[5,64,64]{2,1,0:T(8,128)S(1)}, bf16[5,64,64,256]{3,2,1,0:T(8,128)(2,1)}, s32[5,64]{1,0:T(8,128)S(...) while((s32[]{:T(128)}, f32[5,64,256]{2,1,0:T(8,128)}, ...), condition=%wide.region_9.10_spmd.clone, body=%wide.region_6.9_spmd.sunk.clone | while | flops 58721856 | bytes 17291228 | solution.py:111
  221.1 2.0 gather_fusion
  223.1 1.8 broadcast_select_fusion.3
  225.0 1.7 dynamic-slice_bitcast_fusion.16
  229.0 2.0 gather_fusion
  230.9 1.8 broadcast_select_fusion.3
  232.8 1.7 dynamic-slice_bitcast_fusion.16
  236.8 2.0 gather_fusion
  238.7 1.8 broadcast_select_fusion.3
  240.6 1.7 dynamic-slice_bitcast_fusion.16
  244.6 2.0 gather_fusion
  246.5 1.8 broadcast_select_fusion.3
  248.4 1.7 dynamic-slice_bitcast_fusion.16
  252.4 2.0 gather_fusion
  254.3 1.8 broadcast_select_fusion.3
  256.2 1.7 dynamic-slice_bitcast_fusion.16
  260.8 3.6 all-to-all-start.3
  264.5 7.3 %all-to-all-done.3 = f32[8,40,256]{2,1,0:T(8,128)S(1)} async-done(((f32[8,40,256]{2,1,0:T(8,128)}), f32[8,40,256]{2,1,0:T(8,128)S(1)}, u32[]{:S(2)}, u32[]{:S(2)}) %all-to-all-start.3) | async-done | bytes 327712 | tf_op jit(solution)/shard_map/all_to_all | solution.py:112
  276.0 3.3 all-to-all-start.4
  279.4 4.4 %all-to-all-done.4 = f32[8,40,1]{1,2,0:T(1,128)S(1)} async-done(((f32[8,40,1]{1,2,0:T(1,128)}), f32[8,40,1]{1,2,0:T(1,128)S(1)}, u32[]{:S(2)}, u32[]{:S(2)}) %all-to-all-start.4) | async-done | bytes 1312 | tf_op jit(solution)/shard_map/all_to_all | solution.py:121
  286.3 64.5 %while.26 = (s32[]{:T(128)}, f32[16,16384]{1,0:T(8,128)S(1)}, f32[16,64]{1,0:T(8,128)S(1)}, s32[5,64]{1,0:T(8,128)S(1)}, pred[5,64]{1,0:T(8,128)(4,1)S(1)}, /*in...) while((s32[]{:T(128)}, f32[16,16384]{1,0:T(8,128)S(1)}, ...), condition=%wide.region_17.18_spmd.clone.clone, body=%wide.region_15.17_spmd.clone.sunk.clone | while | flops 259291072 | bytes 34285436 | solution.py:144
  287.4 1.7 dynamic-slice_bitcast_fusion.18
  290.6 4.5 %copy.36 = f32[8,8,64,256]{3,1,2,0:T(8,128)} copy(f32[8,8,64,256]{3,2,1,0:T(8,128)S(1)} %bitcast.145) | data formatting | bytes 8388608 | tf_op jit(solution)/shard_map/while
  295.1 3.8 convolution_add_fusion.6
  300.3 1.7 dynamic-slice_bitcast_fusion.18
  303.5 4.5 %copy.36 = f32[8,8,64,256]{3,1,2,0:T(8,128)} copy(f32[8,8,64,256]{3,2,1,0:T(8,128)S(1)} %bitcast.145) | data formatting | bytes 8388608 | tf_op jit(solution)/shard_map/while
  308.0 3.8 convolution_add_fusion.6
  313.2 1.7 dynamic-slice_bitcast_fusion.18
  316.4 4.5 %copy.36 = f32[8,8,64,256]{3,1,2,0:T(8,128)} copy(f32[8,8,64,256]{3,2,1,0:T(8,128)S(1)} %bitcast.145) | data formatting | bytes 8388608 | tf_op jit(solution)/shard_map/while
  320.9 3.8 convolution_add_fusion.6
  326.1 1.7 dynamic-slice_bitcast_fusion.18
  329.3 4.5 %copy.36 = f32[8,8,64,256]{3,1,2,0:T(8,128)} copy(f32[8,8,64,256]{3,2,1,0:T(8,128)S(1)} %bitcast.145) | data formatting | bytes 8388608 | tf_op jit(solution)/shard_map/while
  333.8 3.8 convolution_add_fusion.6
  342.2 4.5 %copy.36 = f32[8,8,64,256]{3,1,2,0:T(8,128)} copy(f32[8,8,64,256]{3,2,1,0:T(8,128)S(1)} %bitcast.145) | data formatting | bytes 8388608 | tf_op jit(solution)/shard_map/while
  346.7 3.8 convolution_add_fusion.6
  352.9 16.9 %reduce-scatter.7.cloned.1.call-done = f32[16,16]{1,0:T(8,128)} async-done(((f32[64,16]{1,0:T(8,128)}), f32[16,16]{1,0:T(8,128)}) %reduce-scatter.7.cloned.1.call-update) | async-done | bytes 1040
  370.6 26.9 %reduce-scatter.5.cloned.1.call-done = f32[16,16,256]{2,1,0:T(8,128)} async-done(((f32[16,64,256]{2,1,0:T(8,128)}), f32[16,16,256]{2,1,0:T(8,128)}) %reduce-scatter.5.cloned.1.call-update) | async-done | bytes 262160 | tf_op jit(solution)/shard_map/reduce_scatter | solution.py:148
  397.6 1.8 broadcast_divide_fusion
  (152 shorter events, 49.6 us)
Async XLA Ops:
  6.5 33.8 %copy-start = (bf16[32,64,256]{2,1,0:T(8,128)(2,1)S(1)}, bf16[32,64,256]{2,1,0:T(8,128)(2,1)}, u32[]{:S(2)}) copy-start(bf16[32,64,256]{2,1,0:T(8,128)(2,1)} %param.9) | copy-start | bytes 3145732
  34.6 9.8 %all-to-all-start.1 = ((s32[8,40,1]{1,2,0:T(1,128)}), s32[8,40,1]{1,2,0:T(1,128)S(1)}, u32[]{:S(2)}, u32[]{:S(2)}) async-start(s32[8,40,1]{1,2,0:T(1,128)} %bitcast.43), calls=%async_computation.1 | async-start | bytes 8192 | tf_op jit(solution)/shard_map/all_to_all | solution.py:91
  44.4 54.9 %all-to-all-start = ((s32[8,40,1]{1,2,0:T(1,128)}), s32[8,40,1]{1,2,0:T(1,128)S(1)}, u32[]{:S(2)}, u32[]{:S(2)}) async-start(s32[8,40,1]{1,2,0:T(1,128)} %all_to_all.29), calls=%async_computation | async-start | bytes 8192 | tf_op jit(solution)/shard_map/all_to_all | solution.py:90
  99.3 5.3 %copy-start.2 = (bf16[16,64,256]{2,1,0:T(8,128)(2,1)S(1)}, bf16[16,64,256]{2,1,0:T(8,128)(2,1)}, u32[]{:S(2)}) copy-start(bf16[16,64,256]{2,1,0:T(8,128)(2,1)} %param.10) | copy-start | bytes 1572868
  99.3 121.8 %all-to-all-start.2 = ((bf16[320,64,256]{2,1,0:T(8,128)(2,1)}), bf16[320,64,256]{2,1,0:T(8,128)(2,1)}, u32[]{:S(2)}, u32[]{:S(2)}) async-start(bf16[320,64,256]{2,1,0:T(8,128)(2,1)} %scatter_fusion), calls=%async_computation.2 | async-start | bytes 20971520 | tf_op jit(solution)/shard_map/all_to_all | solution.py:89
  104.6 2.5 copy-start.3
  260.1 0.7 copy-start.1
  260.8 11.0 %all-to-all-start.3 = ((f32[8,40,256]{2,1,0:T(8,128)}), f32[8,40,256]{2,1,0:T(8,128)S(1)}, u32[]{:S(2)}, u32[]{:S(2)}) async-start(f32[8,40,256]{2,1,0:T(8,128)} %bitcast.52), calls=%async_computation.3 | async-start | bytes 655360 | tf_op jit(solution)/shard_map/all_to_all | solution.py:112
  276.0 7.9 %all-to-all-start.4 = ((f32[8,40,1]{1,2,0:T(1,128)}), f32[8,40,1]{1,2,0:T(1,128)S(1)}, u32[]{:S(2)}, u32[]{:S(2)}) async-start(f32[8,40,1]{1,2,0:T(1,128)} %all_to_all.37), calls=%async_computation.4 | async-start | bytes 8192 | tf_op jit(solution)/shard_map/all_to_all | solution.py:121
  279.3 90.6 %reduce-scatter.7.cloned.1.call-start = ((), (), s32[]{:S(2)}) async-start(), calls=%async_computation.8 | async-start | bytes 40960
  351.6 46.0 %reduce-scatter.5.cloned.1.call-start = ((), (), s32[]{:S(2)}) async-start(), calls=%async_computation.7 | async-start | bytes 1310720 | tf_op jit(solution)/shard_map/reduce_scatter | solution.py:148
Sparse Core Ops, SparseCore 0:
  351.7 18.1 reduce-scatter.6
  372.3 25.2 reduce-scatter.4
where the time goes:
time: 409 us; the launch traced here: 406 us
  waiting for transfers between devices  171 us (42%)
  local copies, waits for them, and re-layouts  123 us (30%)
  other arithmetic  50.6 us (12%)
  matrix products  26.9 us (7%)
  starting transfers between devices  20.7 us (5%)
  between operations  13.7 us (3%)
    all_to_all x1, waiting for transfers between devices, on_device(): lax.all_to_all(payload, 'cls', split_axis=0, concat_axis=0, tiled=True)  114 us
    scatter x1, local copies, waits for them, and re-layouts, on_device(): payload = jnp.zeros((send_rows, cycle_count, harmonic.shape[2]), jnp.bflo...  37.3 us
    reduce_scatter x1, waiting for transfers between devices, on_device(): lax.psum_scatter(class_sums.reshape(owned, cycle_count, received.shape[2]...  26.9 us
    while x5, local copies, waits for them, and re-layouts  22.3 us
    gather x1, other arithmetic, on_device(): defocus[source]  20.1 us
    dot_general x5, matrix products, add_block(): jnp.dot(member.T, term_rows.reshape(block_rows, -1), precision=lax.Precis...  18.8 us
    squeeze x10, local copies, waits for them, and re-layouts, on_device(): lax.map(score_block, (part_blocks, pick_blocks, ctf_blocks))  17.3 us
    unnamed x3, waiting for transfers between devices  17 us
  transfers between devices with their start and end apart: 7, of which 6 were waited for; matrix products, arithmetic and copies ran while one was open for 15% of the time, Pallas kernels for 0%

commit v1 on v0

v1 whole, which is shorter than its diff:
```python
import functools

import jax
import jax.numpy as jnp
import numpy as np
from jax import lax
from jax.experimental import pallas as pl
from jax.experimental.pallas import tpu as pltpu
from jax.sharding import PartitionSpec as P

MESH = pl.DeviceIdType.MESH
VMEM = pl.BlockSpec(memory_space=pltpu.VMEM)
ANY = pl.BlockSpec(memory_space=pl.ANY)
LIMIT = 56 * 1024 * 1024
F32 = jnp.float32
BF16 = jnp.bfloat16
EXACT = lax.Precision.HIGHEST


def angle_tables(angles):
    harm_count = angles // 2
    phase = np.arange(angles)[:, None] * np.arange(harm_count)[None, :] % angles
    grid = 2.0 * np.pi / angles * phase
    cosine, sine = np.cos(grid), np.sin(grid)
    forward = np.concatenate([cosine, sine], axis=1)
    weight = np.where(np.arange(harm_count) == 0, 1.0, 2.0)[:, None] / angles
    inverse = np.concatenate([cosine.T * weight, -sine.T * weight], axis=0)
    return forward.astype(np.float32), inverse.astype(np.float32)


def compute_call(body, out_shape, inputs, scratch=()):
    return pl.pallas_call(
        body,
        out_shape=out_shape,
        in_specs=[VMEM] * len(inputs),
        out_specs=jax.tree.map(lambda _: VMEM, out_shape),
        scratch_shapes=list(scratch),
        compiler_params=pltpu.CompilerParams(vmem_limit_bytes=LIMIT),
    )(*inputs)


def harmonics_body(owners, cycles, img_ref, ref_ref, table_ref, part_ref, cls_ref, low, high):
    harm = table_ref.shape[1] // 2
    share = cycles // owners
    for src, dst in ((img_ref, part_ref), (ref_ref, cls_ref)):
        rows = src.shape[0]
        frames = rows // cycles
        step = min(256, rows)

        @pl.loop(0, rows // step)
        def _(b):
            at = pl.ds(pl.multiple_of(b * step, step), step)
            out = jnp.dot(src[at, :], table_ref[...], preferred_element_type=F32)
            low[at, :] = out[:, :harm]
            high[at, :] = out[:, harm:]

        for cycle in range(cycles):
            at = pl.ds(cycle, frames, stride=cycles)
            place = cycle % owners * share + cycle // owners
            dst[place, :, :harm] = low[at, :].astype(BF16)
            dst[place, :, harm:] = high[at, :].astype(BF16)


def greet(peers):
    barrier = pltpu.get_barrier_semaphore()
    for peer in peers:
        pl.semaphore_signal(barrier, inc=1, device_id=peer, device_id_type=MESH)
    pl.semaphore_wait(barrier, len(peers))


def exchange_body(owners, spread, *refs):
    count = len(spread)
    ins, outs = refs[:count], refs[count : 2 * count]
    send_sem, recv_sem, local_sem = refs[2 * count :]
    dom, me = lax.axis_index("dom"), lax.axis_index("cls")
    peers = [(dom, lax.rem(me + off, owners)) for off in range(1, owners)]
    greet(peers)
    copies = []
    for off, peer in enumerate(peers, 1):
        for a in range(count):
            copy = pltpu.make_async_remote_copy(
                src_ref=ins[a] if spread[a] else ins[a].at[peer[1]],
                dst_ref=outs[a].at[me],
                send_sem=send_sem.at[off, a],
                recv_sem=recv_sem.at[off, a],
                device_id=peer,
                device_id_type=MESH,
            )
            copy.start()
            copies.append(copy)
    for a in range(count):
        copy = pltpu.make_async_copy(
            ins[a] if spread[a] else ins[a].at[me], outs[a].at[me], local_sem.at[a]
        )
        copy.start()
        copies.append(copy)
    for copy in copies:
        copy.wait()


def exchange(owners, number, arrays, spread):
    count = len(arrays)
    shapes = [
        jax.ShapeDtypeStruct((owners,) + (a.shape if s else a.shape[1:]), a.dtype)
        for a, s in zip(arrays, spread)
    ]
    return pl.pallas_call(
        functools.partial(exchange_body, owners, spread),
        out_shape=shapes,
        in_specs=[ANY] * count,
        out_specs=[ANY] * count,
        scratch_shapes=[
            pltpu.SemaphoreType.DMA((owners, count)),
            pltpu.SemaphoreType.DMA((owners, count)),
            pltpu.SemaphoreType.DMA((count,)),
        ],
        compiler_params=pltpu.CompilerParams(collective_id=number, has_side_effects=True),
    )(*arrays)


def ctf_rows(meta, priors, table_ref):
    groups = table_ref.shape[0]
    group = meta[:, priors : priors + 1]
    hits = (group == lax.broadcasted_iota(jnp.int32, (meta.shape[0], groups), 1)).astype(F32)
    return jnp.dot(hits, table_ref[...], precision=EXACT, preferred_element_type=F32)


def column(rows, index):
    lanes = lax.broadcasted_iota(jnp.int32, rows.shape, 1)
    return jnp.sum(jnp.where(lanes == index, rows, 0.0), axis=1, keepdims=True)


def weighted_parts(part_ref, ctf, owners, scaled):
    me = lax.axis_index("cls")
    share = part_ref.shape[1]
    for i in range(share):
        frames = part_ref[:, i].reshape(-1, part_ref.shape[3]).astype(F32)
        scaled[i] = frames * column(ctf, me + owners * i)


def class_hits(meta, j, classes):
    picked = column(meta.astype(F32), j)
    lanes = lax.broadcasted_iota(jnp.int32, (meta.shape[0], classes), 1)
    return (picked.astype(jnp.int32) == lanes).astype(F32)


def score_body(owners, priors, part_ref, cls_ref, meta_ref, table_ref, out_ref, scaled):
    share, width = part_ref.shape[1], part_ref.shape[3]
    harm = width // 2
    classes = owners * cls_ref.shape[2]
    frames = part_ref.shape[2]
    meta = meta_ref[...].reshape(-1, meta_ref.shape[2])
    weighted_parts(part_ref, ctf_rows(meta, priors, table_ref), owners, scaled)

    @pl.loop(0, priors)
    def _(j):
        hits = class_hits(meta_ref[...].reshape(-1, meta_ref.shape[2]), j, classes).astype(BF16)
        real, imag = 0.0, 0.0
        for i in range(share):
            picked = jnp.dot(
                hits, cls_ref[:, i].reshape(classes, width), preferred_element_type=F32
            )
            pc, ps = scaled[i, :, :harm], scaled[i, :, harm:]
            cc, cs = picked[:, :harm], picked[:, harm:]
            real = real + (pc * cc + ps * cs)
            imag = imag + (pc * cs - ps * cc)
        out_ref[:, j, :, :harm] = real.astype(BF16).reshape(owners, frames, harm)
        out_ref[:, j, :, harm:] = imag.astype(BF16).reshape(owners, frames, harm)


def weight_body(owners, got_ref, forward_ref, inverse_ref, out_ref):
    priors, frames, width = got_ref.shape[1:]
    joined = got_ref[0].astype(F32)
    for src in range(1, owners):
        joined = joined + got_ref[src].astype(F32)
    joined = joined.reshape(priors * frames, width)
    scores = jnp.dot(joined, inverse_ref[...], precision=EXACT, preferred_element_type=F32)
    scores = scores.reshape(priors, frames, -1)
    highest = jnp.max(jnp.max(scores, axis=0), axis=1, keepdims=True)
    total = jnp.sum(jnp.sum(jnp.exp(scores - highest[None]), axis=0), axis=1, keepdims=True)
    log_total = highest + jnp.log(total)
    weights = jnp.exp(scores - log_total[None]).reshape(priors * frames, -1)
    spectrum = jnp.dot(weights, forward_ref[...], precision=EXACT, preferred_element_type=F32)
    out_ref[...] = spectrum.astype(BF16).reshape(out_ref.shape)


def sum_body(
    owners, priors, spec_ref, part_ref, meta_ref, table_ref, out_ref, norm_ref, scaled, sums, norms
):
    share, width = part_ref.shape[1], part_ref.shape[3]
    harm = width // 2
    owned = norm_ref.shape[0]
    classes = owners * owned
    meta = meta_ref[...].reshape(-1, meta_ref.shape[2])
    ctf = ctf_rows(meta, priors, table_ref)
    weighted_parts(part_ref, ctf, owners, scaled)
    ctf_square = ctf * ctf
    sums[...] = jnp.zeros_like(sums)
    norms[...] = jnp.zeros_like(norms)

    @pl.loop(0, priors)
    def _(j):
        hits = class_hits(meta_ref[...].reshape(-1, meta_ref.shape[2]), j, classes).T
        spectrum = spec_ref[:, j].reshape(-1, width).astype(F32)
        wc, ws = spectrum[:, :harm], spectrum[:, harm:]
        norms[...] += jnp.dot(
            hits, ctf_square * wc[:, :1], precision=EXACT, preferred_element_type=F32
        )
        hits = hits.astype(BF16)
        for i in range(share):
            pc, ps = scaled[i, :, :harm], scaled[i, :, harm:]
            terms = jnp.concatenate([pc * wc + ps * ws, ps * wc - pc * ws], axis=1)
            sums[i] += jnp.dot(hits, terms.astype(BF16), preferred_element_type=F32)

    out_ref[...] = sums[...].astype(BF16)
    mine = pl.multiple_of(lax.axis_index("cls") * owned, owned)
    norm_ref[...] = norms[pl.ds(mine, owned), :]


def deliver_body(doms, owners, sum_ref, norm_ref, got_ref, norm_got, sems, norm_sems, local):
    run, owned = got_ref.shape[1:3]
    dom, me = lax.axis_index("dom"), lax.axis_index("cls")
    offsets = [(a, b) for a in range(doms) for b in range(owners) if (a, b) != (0, 0)]
    peers = [(lax.rem(dom + a, doms), lax.rem(me + b, owners)) for a, b in offsets]
    greet(peers)

    def block(index):
        start = pl.multiple_of(index[1] * owned, owned)
        return sum_ref.at[pl.ds(index[0] * run, run), pl.ds(start, owned), :]

    copies = []
    for (a, b), peer in zip(offsets, peers):
        copies.append(
            pltpu.make_async_remote_copy(
                src_ref=block(peer),
                dst_ref=got_ref.at[dom * owners + me],
                send_sem=sems.at[0, a, b],
                recv_sem=sems.at[1, a, b],
                device_id=peer,
                device_id_type=MESH,
            )
        )
        if b == 0:
            copies.append(
                pltpu.make_async_remote_copy(
                    src_ref=norm_ref,
                    dst_ref=norm_got.at[dom],
                    send_sem=norm_sems.at[0, a],
                    recv_sem=norm_sems.at[1, a],
                    device_id=peer,
                    device_id_type=MESH,
                )
            )
    copies.append(
        pltpu.make_async_copy(block((dom, me)), got_ref.at[dom * owners + me], local.at[0])
    )
    copies.append(pltpu.make_async_copy(norm_ref, norm_got.at[dom], local.at[1]))
    for copy in copies:
        copy.start()
    for copy in copies:
        copy.wait()


def deliver(doms, owners, sums, norms):
    share, classes, width = sums.shape
    owned = norms.shape[0]
    run = share // doms
    return pl.pallas_call(
        functools.partial(deliver_body, doms, owners),
        out_shape=[
            jax.ShapeDtypeStruct((doms * owners, run, owned, width), BF16),
            jax.ShapeDtypeStruct((doms,) + norms.shape, F32),
        ],
        in_specs=[ANY] * 2,
        out_specs=[ANY] * 2,
        scratch_shapes=[
            pltpu.SemaphoreType.DMA((2, doms, owners)),
            pltpu.SemaphoreType.DMA((2, doms)),
            pltpu.SemaphoreType.DMA((2,)),
        ],
        compiler_params=pltpu.CompilerParams(collective_id=4, has_side_effects=True),
    )(sums, norms)


def finish_body(doms, owners, got_ref, norm_ref, out_ref, low, high):
    run, owned, width = got_ref.shape[1:]
    harm = width // 2
    held = run * owners
    norms = norm_ref[0]
    for a in range(1, doms):
        norms = norms + norm_ref[a]
    first = lax.axis_index("dom") * held
    for i in range(run):
        for c in range(owners):
            total = got_ref[c, i].astype(F32)
            for a in range(1, doms):
                total = total + got_ref[a * owners + c, i].astype(F32)
            cycle = c + owners * i
            result = total / (column(norms, first + cycle) + 1.0)
            at = pl.ds(cycle, owned, stride=held)
            low[at, :] = result[:, :harm]
            high[at, :] = result[:, harm:]
    out_ref[:, :harm] = low[...]
    out_ref[:, harm:] = high[...]


def on_device(doms, images, references, ctf_table, defocus, priors):
    owners = lax.axis_size("cls")
    particles, cycles, angles = images.shape
    owned = references.shape[0]
    classes = owners * owned
    prior_count = priors.shape[1]
    share = cycles // owners
    width = angles // 2 * 2
    group = owners * particles
    forward, inverse = (jnp.asarray(t) for t in angle_tables(angles))
    meta = jnp.concatenate(
        [priors, defocus[:, None], jnp.zeros((particles, 127 - prior_count), jnp.int32)], axis=1
    )

    part_send, cls_send = compute_call(
        functools.partial(harmonics_body, owners, cycles),
        [
            jax.ShapeDtypeStruct((cycles, particles, width), BF16),
            jax.ShapeDtypeStruct((cycles, owned, width), BF16),
        ],
        (
            images.reshape(particles * cycles, angles),
            references.reshape(owned * cycles, angles),
            forward.astype(BF16),
        ),
        [pltpu.VMEM((max(particles, owned) * cycles, width // 2), F32)] * 2,
    )
    part, cls, meta = exchange(
        owners,
        1,
        (
            part_send.reshape(owners, share, particles, width),
            cls_send.reshape(owners, share, owned, width),
            meta,
        ),
        (False, False, True),
    )
    partial = compute_call(
        functools.partial(score_body, owners, prior_count),
        jax.ShapeDtypeStruct((owners, prior_count, particles, width), BF16),
        (part, cls, meta, ctf_table),
        [pltpu.VMEM((share, group, width), F32)],
    )
    (got,) = exchange(owners, 2, (partial,), (False,))
    spectrum = compute_call(
        functools.partial(weight_body, owners),
        jax.ShapeDtypeStruct((prior_count, particles, width), BF16),
        (got, forward, inverse),
    )
    (spectra,) = exchange(owners, 3, (spectrum,), (True,))
    sums, norms = compute_call(
        functools.partial(sum_body, owners, prior_count),
        [
            jax.ShapeDtypeStruct((share, classes, width), BF16),
            jax.ShapeDtypeStruct((owned, cycles), F32),
        ],
        (spectra, part, meta, ctf_table),
        [
            pltpu.VMEM((share, group, width), F32),
            pltpu.VMEM((share, classes, width), F32),
            pltpu.VMEM((classes, cycles), F32),
        ],
    )
    held = cycles // doms
    if held % owners == 0:
        norms = jnp.pad(norms, ((0, 0), (0, 128 - cycles)))
        got, norms = deliver(doms, owners, sums, norms)
        out = compute_call(
            functools.partial(finish_body, doms, owners),
            jax.ShapeDtypeStruct((owned * held, width), F32),
            (got, norms),
            [pltpu.VMEM((owned * held, width // 2), F32)] * 2,
        )
        return out.reshape(owned, held, width)
    mine = lax.axis_index("cls") + owners * jnp.arange(share)
    placed = jnp.zeros((cycles, classes, width), F32).at[mine].set(sums.astype(F32))
    placed = lax.psum_scatter(placed, "dom", scatter_dimension=0, tiled=True)
    placed = lax.psum_scatter(placed, "cls", scatter_dimension=1, tiled=True)
    norms = lax.psum_scatter(norms, "dom", scatter_dimension=1, tiled=True)
    return placed.transpose(1, 0, 2) / (norms + 1.0)[:, :, None]


def solution(mesh):
    return jax.shard_map(
        functools.partial(on_device, mesh.shape["dom"]),
        mesh=mesh,
        in_specs=(
            P(("dom", "cls"), None, None),
            P("cls", None, None),
            P(),
            P(("dom", "cls")),
            P(("dom", "cls"), None),
        ),
        out_specs=P("cls", "dom", None),
        check_vma=False,
    )
```

time: 409 us -> 103 us (0.25)
  waiting for transfers between devices: 171 us -> 0 us
  local copies, waits for them, and re-layouts: 123 us -> 2.69 us
  Pallas kernels: 0 us -> 98.6 us
  other arithmetic: 50.6 us -> 0.68 us
  matrix products: 26.9 us -> 0 us
  starting transfers between devices: 20.7 us -> 0 us
  between operations: 13.7 us -> 0.04 us
    all_to_all x5 -> x0, waiting for transfers between devices: 127 us -> none  [the longest x1 114 us: on_device(): lax.all_to_all(payload, 'cls', split_axis=0, concat_axis=0, tiled=True)]
    pallas_call x0 -> x9, Pallas kernels: none -> 98.6 us  [the longest x3 53.6 us: exchange(): pl.pallas_call(functools.partial(exchange_body, owners, spread), out_shap...]
    scatter x4 -> x0, local copies, waits for them, and re-layouts: 41.5 us -> none  [the longest x1 37.3 us: on_device(): payload = jnp.zeros((send_rows, cycle_count, harmonic.shape[2]), jnp.bflo...]
    reduce_scatter x1 -> x0, waiting for transfers between devices: 26.9 us -> none  [on_device(): lax.psum_scatter(class_sums.reshape(owned, cycle_count, received.shape[2]...]
    dot_general x23 -> x0, matrix products: 26.9 us -> none  [the longest x5 18.8 us: add_block(): jnp.dot(member.T, term_rows.reshape(block_rows, -1), precision=lax.Precis...]
    gather x9 -> x0, local copies, waits for them, and re-layouts: 23.4 us -> none  [the longest x5 9.87 us: score_block(): jnp.take(ref_harm, pick_block, axis=0)]
    while x5 -> x0, local copies, waits for them, and re-layouts: 22.3 us -> none
    all_to_all x5 -> x0, starting transfers between devices: 20.6 us -> none  [the longest x1 5.27 us: on_device(): lax.all_to_all(payload, 'cls', split_axis=0, concat_axis=0, tiled=True)]
  transfers between devices with their start and end apart: 7 -> 0, of which waited for: 6 -> 0; matrix products, arithmetic and copies ran while one was open for 15% -> 0% of each run, Pallas kernels for 0% -> 0%
where the time goes in v1:
time: 103 us; the launch traced here: 102 us
  Pallas kernels  98.6 us (96%)
  local copies, waits for them, and re-layouts  2.69 us (3%)
    pallas_call x3, Pallas kernels, exchange(): pl.pallas_call(functools.partial(exchange_body, owners, spread), out_shap...  53.6 us
    pallas_call x5, Pallas kernels, compute_call(): pl.pallas_call(body, out_shape=out_shape, in_specs=[VMEM] * len(inputs),...  27.6 us
    pallas_call x1, Pallas kernels, deliver(): pl.pallas_call(functools.partial(deliver_body, doms, owners), out_shape=[...  17.3 us

profile of v1, /device:TPU:0, one launch (start us, length us, event | category | flops | bytes accessed | tf_op | source)
XLA Modules:
  0.0 102.0 jit_solution(494815045440124841)
XLA Ops:
  0.0 0.0 copy-start.1
  0.0 0.1 pad.7.clone
  0.1 0.6 copy-done.1
  0.7 0.0 copy-start
  0.7 0.1 copy.9
  0.7 0.6 copy-done
  1.3 0.1 copy.8
  1.4 0.7 add_add_fusion.refs_2_
  2.1 6.3 %shard_map.73 = (bf16[64,32,256]{2,1,0:T(8,128)(2,1)}, bf16[64,16,256]{2,1,0:T(8,128)(2,1)}) custom-call(bf16[2048,256]{1,0:T(8,128)(2,1)} %bitcast.7, bf16[1024,256]{1,0:T(8,128)(2,1)} %bitcast.9, bf16[256,256]{1,0:T(8,128)(2,1)} %constant.13.table_ref), custom_call_target="tpu_custom_call" | custom-call | tf_op jit(solution)/shard_map/pallas_call | solution.py:32
  8.4 23.4 %shard_map.74 = (bf16[8,8,32,256]{3,2,1,0:T(8,128)(2,1)}, bf16[8,8,16,256]{3,2,1,0:T(8,128)(2,1)}, s32[8,32,128]{2,1,0:T(8,128)}) custom-call(bf16[8,8,32,256]{3,2,1,0:T(8,128)(2,1)} %bitcast.6, bf16[8,8,16,256]{3,2,1,0:T(8,128)(2,1)} %bitcast.8, s32[32,128]{1,0:T(8,128)} %add_add_fusion.refs_2_), custom_call_target="tpu_custom_call" | custom-call | tf_op jit(solution)/shard_map/pallas_call | solution.py:107
  31.8 7.1 %shard_map.75.refs_0_ = bf16[8,8,32,256]{3,2,1,0:T(8,128)(2,1)} custom-call(bf16[8,8,32,256]{3,2,1,0:T(8,128)(2,1)} %get-tuple-element.16.part_ref, bf16[8,8,16,256]{3,2,1,0:T(8,128)(2,1)} %get-tuple-element.17.cls_ref, s32[8,32,128]{2,1,0:T(8,128)} %get-tuple-element.18.meta_ref, f32[64,64]{1,0:T(8,128)} %table_ref.3), custom_call_target="tpu_custom_call" | custom-call | tf_op jit(solution)/shard_map/pallas_call | solution.py:32
  38.9 15.1 %shard_map.76.got_ref = bf16[8,8,32,256]{3,2,1,0:T(8,128)(2,1)} custom-call(bf16[8,8,32,256]{3,2,1,0:T(8,128)(2,1)} %shard_map.75.refs_0_), custom_call_target="tpu_custom_call" | custom-call | tf_op jit(solution)/shard_map/pallas_call | solution.py:107
  54.0 3.4 %shard_map.77.refs_0_ = bf16[8,32,256]{2,1,0:T(8,128)(2,1)} custom-call(bf16[8,8,32,256]{3,2,1,0:T(8,128)(2,1)} %shard_map.76.got_ref, f32[256,256]{1,0:T(8,128)} %constant.9.clone.forward_ref, f32[256,256]{1,0:T(8,128)} %constant.10.clone.inverse_ref), custom_call_target="tpu_custom_call" | custom-call | tf_op jit(solution)/shard_map/pallas_call | solution.py:32
  57.4 15.1 %shard_map.78.spec_ref = bf16[8,8,32,256]{3,2,1,0:T(8,128)(2,1)} custom-call(bf16[8,32,256]{2,1,0:T(8,128)(2,1)} %shard_map.77.refs_0_), custom_call_target="tpu_custom_call" | custom-call | tf_op jit(solution)/shard_map/pallas_call | solution.py:107
  72.5 8.9 %shard_map.79 = (bf16[8,128,256]{2,1,0:T(8,128)(2,1)}, f32[16,64]{1,0:T(8,128)}) custom-call(bf16[8,8,32,256]{3,2,1,0:T(8,128)(2,1)} %shard_map.78.spec_ref, bf16[8,8,32,256]{3,2,1,0:T(8,128)(2,1)} %get-tuple-element.16.part_ref, s32[8,32,128]{2,1,0:T(8,128)} %get-tuple-element.18.meta_ref, f32[64,64]{1,0:T(8,128)} %table_ref.3), custom_call_target="tpu_custom_call" | custom-call | tf_op jit(solution)/shard_map/pallas_call | solution.py:32
  81.4 1.3 %pad.4.norm_ref = f32[16,128]{1,0:T(8,128)} pad(f32[16,64]{1,0:T(8,128)} %get-tuple-element.20, f32[]{:T(128)} %constant.8.clone.1), padding=0_0x0_64 | pad | bytes 12292 | tf_op jit(solution)/shard_map/jit(_pad)/pad | solution.py:372
  82.6 17.3 %shard_map.80 = (bf16[32,2,16,256]{3,2,1,0:T(8,128)(2,1)}, f32[4,16,128]{2,1,0:T(8,128)}) custom-call(bf16[8,128,256]{2,1,0:T(8,128)(2,1)} %get-tuple-element.19.sum_ref, f32[16,128]{1,0:T(8,128)} %pad.4.norm_ref), custom_call_target="tpu_custom_call" | custom-call | tf_op jit(solution)/shard_map/pallas_call | solution.py:268
  100.0 2.0 %shard_map.81 = f32[256,256]{1,0:T(8,128)} custom-call(bf16[32,2,16,256]{3,2,1,0:T(8,128)(2,1)} %get-tuple-element.21.got_ref, f32[4,16,128]{2,1,0:T(8,128)} %get-tuple-element.22.norm_ref), custom_call_target="tpu_custom_call" | custom-call | tf_op jit(solution)/shard_map/pallas_call | solution.py:32
  (1 shorter events, 0.0 us)
Async XLA Ops:
  0.0 0.7 copy-start.1
  0.7 0.7 copy-start

commit v2 on v0

v2 whole, which is shorter than its diff:
```python
import functools

import jax
import jax.numpy as jnp
import numpy as np
from jax import lax
from jax.experimental import pallas as pl
from jax.experimental.pallas import tpu as pltpu
from jax.sharding import PartitionSpec as P

MESH = pl.DeviceIdType.MESH
VMEM = pl.BlockSpec(memory_space=pltpu.VMEM)
LIMIT = 56 * 1024 * 1024
F32 = jnp.float32
BF16 = jnp.bfloat16
EXACT = lax.Precision.HIGHEST
TILE = 16


def angle_tables(angles):
    harm_count = angles // 2
    phase = np.arange(angles)[:, None] * np.arange(harm_count)[None, :] % angles
    grid = 2.0 * np.pi / angles * phase
    cosine, sine = np.cos(grid), np.sin(grid)
    forward = np.concatenate([cosine, sine], axis=1)
    weight = np.where(np.arange(harm_count) == 0, 1.0, 2.0)[:, None] / angles
    inverse = np.concatenate([cosine.T * weight, -sine.T * weight], axis=0)
    return forward.astype(np.float32), inverse.astype(np.float32)


def swap_matrix():
    rows = np.arange(TILE * TILE)
    swap = np.zeros((TILE * TILE, TILE * TILE), np.float32)
    swap[rows, rows % TILE * TILE + rows // TILE] = 1.0
    return swap


def harmonics(src, dst, swap, table, owners):
    frames, cycles, angles = src.shape
    for first in range(0, cycles, TILE):
        for frame in range(0, frames, TILE):
            block = src[frame : frame + TILE, first : first + TILE, :]
            block = block.reshape(TILE * TILE, angles)
            block = jnp.dot(swap, block, preferred_element_type=F32).astype(BF16)
            out = jnp.dot(block, table, preferred_element_type=F32).astype(BF16)
            for r in range(TILE):
                cycle = first + r
                dst[cycle % owners, cycle // owners, frame : frame + TILE, :] = out[
                    r * TILE : (r + 1) * TILE
                ]


def column(rows, index):
    lanes = lax.broadcasted_iota(jnp.int32, rows.shape, 1)
    return jnp.sum(jnp.where(lanes == index, rows, 0.0), axis=1, keepdims=True)


def class_hits(meta, priors, classes):
    lanes = lax.broadcasted_iota(jnp.int32, (meta.shape[0], classes), 1)
    return jnp.concatenate(
        [(meta[:, j : j + 1] == lanes).astype(F32) for j in range(priors)], axis=0
    )


def ctf_rows(meta, priors, table):
    groups = table.shape[0]
    lanes = lax.broadcasted_iota(jnp.int32, (meta.shape[0], groups), 1)
    hits = (meta[:, priors : priors + 1] == lanes).astype(F32)
    return jnp.dot(hits, table, precision=EXACT, preferred_element_type=F32)


def body(
    doms,
    owners,
    priors,
    deliver,
    img_ref,
    ref_ref,
    meta_ref,
    ctf_ref,
    swap_ref,
    forward_ref,
    inverse_ref,
    *rest,
):
    if deliver:
        out_ref, rest = rest[0], rest[1:]
    else:
        sum_out, norm_out, rest = rest[0], rest[1], rest[2:]
    (
        part_send,
        part_got,
        cls_send,
        cls_got,
        meta_got,
        scaled,
        ctf_got,
        score_send,
        score_got,
        spec_send,
        spec_got,
        sums,
        norms,
        sum_send,
        sum_got,
        norm_send,
        norm_got,
        low,
        high,
        cls_sem,
        meta_sem,
        part_sem,
        score_sem,
        spec_sem,
        sum_sem,
        norm_sem,
    ) = rest
    dom, me = lax.axis_index("dom"), lax.axis_index("cls")
    particles, cycles, angles = img_ref.shape
    owned = ref_ref.shape[0]
    classes = owners * owned
    share = cycles // owners
    harm = angles // 2
    width = 2 * harm

    barrier = pltpu.get_barrier_semaphore()
    offsets = [(a, b) for a in range(doms if deliver else 1) for b in range(owners)][1:]

    def peer(a, b):
        return (lax.rem(dom + a, doms), lax.rem(me + b, owners))

    def remote(src, dst, sem, place, device):
        return pltpu.make_async_remote_copy(
            src_ref=src,
            dst_ref=dst,
            send_sem=sem.at[(0,) + place],
            recv_sem=sem.at[(1,) + place],
            device_id=device,
            device_id_type=MESH,
        )

    def cls_copy(off):
        to = peer(0, off)
        return remote(cls_send.at[to[1]], cls_got.at[me], cls_sem, (off,), to)

    def meta_copy(off):
        return remote(meta_ref, meta_got.at[me], meta_sem, (off,), peer(0, off))

    def part_copy(off):
        to = peer(0, off)
        return remote(part_send.at[to[1]], part_got.at[me], part_sem, (off,), to)

    def score_copy(off):
        to = peer(0, owners - off)
        return remote(score_send.at[to[1]], score_got.at[me], score_sem, (off,), to)

    def spec_copy(off):
        return remote(spec_send, spec_got.at[me], spec_sem, (off,), peer(0, off))

    for a, b in offsets:
        pl.semaphore_signal(barrier, inc=1, device_id=peer(a, b), device_id_type=MESH)
    table = forward_ref[...].astype(BF16)
    swap = swap_ref[...]
    harmonics(ref_ref, cls_send, swap, table, owners)
    pl.semaphore_wait(barrier, len(offsets))
    for off in range(1, owners):
        meta_copy(off).start()
        cls_copy(off).start()
    harmonics(img_ref, part_send, swap, table, owners)
    for off in range(1, owners):
        part_copy(off).start()
    cls_got[me] = cls_send[me]
    part_got[me] = part_send[me]
    meta_got[me] = meta_ref[...]

    def score(src):
        meta = meta_got[src]
        ctf = ctf_rows(meta, priors, ctf_ref[...])
        ctf_got[src] = ctf
        hits = class_hits(meta, priors, classes).astype(BF16)
        real, imag = 0.0, 0.0
        for i in range(share):
            part = part_got[src, i].astype(F32) * column(ctf, me + owners * i)
            scaled[src, i] = part
            table = cls_got[:, i].reshape(classes, width)
            picked = jnp.dot(hits, table, preferred_element_type=F32)
            picked = picked.reshape(priors, particles, width)
            pc, ps = part[None, :, :harm], part[None, :, harm:]
            cc, cs = picked[:, :, :harm], picked[:, :, harm:]
            real = real + (pc * cc + ps * cs)
            imag = imag + (pc * cs - ps * cc)
        score_send[src, :, :, :harm] = real.astype(BF16)
        score_send[src, :, :, harm:] = imag.astype(BF16)

    for off in range(1, owners):
        meta_copy(off).wait()
        cls_copy(off).wait()

    @pl.loop(1, owners)
    def _(off):
        part_copy(off).wait_recv()
        score(lax.rem(me - off + owners, owners))
        score_copy(off).start()

    score(me)

    joined = score_send[me].astype(F32)
    for off in range(1, owners):
        score_copy(off).wait_recv()
        joined = joined + score_got[lax.rem(me + off, owners)].astype(F32)
    joined = joined.reshape(priors * particles, width)
    scores = jnp.dot(joined, inverse_ref[...], precision=EXACT, preferred_element_type=F32)
    scores = scores.reshape(priors, particles, angles)
    highest = jnp.max(jnp.max(scores, axis=0), axis=1, keepdims=True)
    total = jnp.sum(jnp.sum(jnp.exp(scores - highest[None]), axis=0), axis=1, keepdims=True)
    log_total = highest + jnp.log(total)
    weights = jnp.exp(scores - log_total[None]).reshape(priors * particles, angles)
    spectrum = jnp.dot(weights, forward_ref[...], precision=EXACT, preferred_element_type=F32)
    spec_send[...] = spectrum.astype(BF16).reshape(spec_send.shape)
    for off in range(1, owners):
        spec_copy(off).start()
    spec_got[me] = spec_send[...]
    sums[...] = jnp.zeros_like(sums)
    norms[...] = jnp.zeros_like(norms)

    def add(src):
        hits = class_hits(meta_got[src], priors, classes).T
        spectrum = spec_got[src].astype(F32)
        wc, ws = spectrum[:, :, :harm], spectrum[:, :, harm:]
        ctf = ctf_got[src]
        square = (ctf * ctf)[None] * wc[:, :, :1]
        norms[...] += jnp.dot(
            hits,
            square.reshape(priors * particles, cycles),
            precision=EXACT,
            preferred_element_type=F32,
        )
        hits = hits.astype(BF16)
        for i in range(share):
            part = scaled[src, i][None]
            pc, ps = part[:, :, :harm], part[:, :, harm:]
            terms = jnp.concatenate([pc * wc + ps * ws, ps * wc - pc * ws], axis=2)
            terms = terms.reshape(priors * particles, width).astype(BF16)
            sums[i] += jnp.dot(hits, terms, preferred_element_type=F32)

    add(me)

    @pl.loop(1, owners)
    def _(off):
        spec_copy(off).wait_recv()
        add(lax.rem(me - off + owners, owners))

    for off in range(1, owners):
        part_copy(off).wait_send()
        score_copy(off).wait_send()
        spec_copy(off).wait_send()

    mine = pl.multiple_of(me * owned, owned)
    if not deliver:
        sum_out[...] = sums[...].astype(BF16)
        norm_out[...] = norms[pl.ds(mine, owned), :]
        return

    run = share // doms
    held = cycles // doms
    sum_send[...] = sums[...].astype(BF16)
    norm_send[:, :cycles] = norms[pl.ds(mine, owned), :]

    def sum_copy(a, b):
        to = peer(a, b)
        start = pl.multiple_of(to[1] * owned, owned)
        src = sum_send.at[pl.ds(to[0] * run, run), pl.ds(start, owned), :]
        return remote(src, sum_got.at[dom, me], sum_sem, (a, b), to)

    def norm_copy(a):
        return remote(norm_send, norm_got.at[dom], norm_sem, (a,), peer(a, 0))

    order = sorted(offsets, key=lambda o: (o[0] == 0, abs(o[0] - doms // 2)))
    for a, b in order:
        sum_copy(a, b).start()
        if b == 0:
            norm_copy(a).start()
    sum_got[dom, me] = sum_send[pl.ds(dom * run, run), pl.ds(mine, owned), :]
    norm_got[dom] = norm_send[...]
    for a, b in offsets:
        sum_copy(a, b).wait()
        if b == 0:
            norm_copy(a).wait()
    total_norm = norm_got[0, :, :cycles]
    for a in range(1, doms):
        total_norm = total_norm + norm_got[a, :, :cycles]
    for i in range(run):
        for c in range(owners):
            cycle = c + owners * i
            result = sum_got[0, c, i].astype(F32)
            for a in range(1, doms):
                result = result + sum_got[a, c, i].astype(F32)
            result = result / (column(total_norm, dom * held + cycle) + 1.0)
            at = pl.ds(cycle, owned, stride=held)
            low[at, :] = result[:, :harm]
            high[at, :] = result[:, harm:]
    out_ref[:, :harm] = low[...]
    out_ref[:, harm:] = high[...]


def on_device(doms, images, references, ctf_table, defocus, priors):
    owners = lax.axis_size("cls")
    particles, cycles, angles = images.shape
    owned = references.shape[0]
    classes = owners * owned
    prior_count = priors.shape[1]
    share = cycles // owners
    width = angles // 2 * 2
    held = cycles // doms
    deliver = held % owners == 0
    run = max(share // doms, 1)
    forward, inverse = (jnp.asarray(t) for t in angle_tables(angles))
    swap = jnp.asarray(swap_matrix(), BF16)
    meta = jnp.concatenate(
        [priors, defocus[:, None], jnp.zeros((particles, 127 - prior_count), jnp.int32)], axis=1
    )
    if deliver:
        shapes = [jax.ShapeDtypeStruct((owned * held, width), F32)]
    else:
        shapes = [
            jax.ShapeDtypeStruct((share, classes, width), BF16),
            jax.ShapeDtypeStruct((owned, cycles), F32),
        ]
    slots = (prior_count, particles, width)
    sums = (share, classes, width)
    done = pl.pallas_call(
        functools.partial(body, doms, owners, prior_count, deliver),
        out_shape=shapes,
        in_specs=[VMEM] * 7,
        out_specs=[VMEM] * len(shapes),
        scratch_shapes=[
            pltpu.VMEM((owners, share, particles, width), BF16),
            pltpu.VMEM((owners, share, particles, width), BF16),
            pltpu.VMEM((owners, share, owned, width), BF16),
            pltpu.VMEM((owners, share, owned, width), BF16),
            pltpu.VMEM((owners,) + meta.shape, jnp.int32),
            pltpu.VMEM((owners, share, particles, width), F32),
            pltpu.VMEM((owners, particles, cycles), F32),
            pltpu.VMEM((owners,) + slots, BF16),
            pltpu.VMEM((owners,) + slots, BF16),
            pltpu.VMEM(slots, BF16),
            pltpu.VMEM((owners,) + slots, BF16),
            pltpu.VMEM(sums, F32),
            pltpu.VMEM((classes, cycles), F32),
            pltpu.VMEM(sums, BF16),
            pltpu.VMEM((doms, owners, run, owned, width), BF16),
            pltpu.VMEM((owned, 128), F32),
            pltpu.VMEM((doms, owned, 128), F32),
            pltpu.VMEM((owned * held, width // 2), F32),
            pltpu.VMEM((owned * held, width // 2), F32),
            pltpu.SemaphoreType.DMA((2, owners)),
            pltpu.SemaphoreType.DMA((2, owners)),
            pltpu.SemaphoreType.DMA((2, owners)),
            pltpu.SemaphoreType.DMA((2, owners)),
            pltpu.SemaphoreType.DMA((2, owners)),
            pltpu.SemaphoreType.DMA((2, doms, owners)),
            pltpu.SemaphoreType.DMA((2, doms)),
        ],
        compiler_params=pltpu.CompilerParams(
            collective_id=1, has_side_effects=True, vmem_limit_bytes=LIMIT
        ),
    )(images, references, meta, ctf_table, swap, forward, inverse)
    if deliver:
        return done[0].reshape(owned, held, width)
    sums, norms = done
    mine = lax.axis_index("cls") + owners * jnp.arange(share)
    placed = jnp.zeros((cycles, classes, width), F32).at[mine].set(sums.astype(F32))
    placed = lax.psum_scatter(placed, "dom", scatter_dimension=0, tiled=True)
    placed = lax.psum_scatter(placed, "cls", scatter_dimension=1, tiled=True)
    norms = lax.psum_scatter(norms, "dom", scatter_dimension=1, tiled=True)
    return placed.transpose(1, 0, 2) / (norms + 1.0)[:, :, None]


def solution(mesh):
    return jax.shard_map(
        functools.partial(on_device, mesh.shape["dom"]),
        mesh=mesh,
        in_specs=(
            P(("dom", "cls"), None, None),
            P("cls", None, None),
            P(),
            P(("dom", "cls")),
            P(("dom", "cls"), None),
        ),
        out_specs=P("cls", "dom", None),
        check_vma=False,
    )
```

time: 409 us -> 71.5 us (0.17)
  waiting for transfers between devices: 171 us -> 0 us
  local copies, waits for them, and re-layouts: 123 us -> 3.09 us
  Pallas kernels: 0 us -> 66.7 us
  other arithmetic: 50.6 us -> 0.68 us
  matrix products: 26.9 us -> 0 us
  starting transfers between devices: 20.7 us -> 0 us
  between operations: 13.7 us -> 0.01 us
    all_to_all x5 -> x0, waiting for transfers between devices: 127 us -> none  [the longest x1 114 us: on_device(): lax.all_to_all(payload, 'cls', split_axis=0, concat_axis=0, tiled=True)]
    pallas_call x0 -> x1, Pallas kernels: none -> 66.7 us  [on_device(): pl.pallas_call(functools.partial(body, doms, owners, prior_count, deliver...]
    scatter x4 -> x0, local copies, waits for them, and re-layouts: 41.5 us -> none  [the longest x1 37.3 us: on_device(): payload = jnp.zeros((send_rows, cycle_count, harmonic.shape[2]), jnp.bflo...]
    reduce_scatter x1 -> x0, waiting for transfers between devices: 26.9 us -> none  [on_device(): lax.psum_scatter(class_sums.reshape(owned, cycle_count, received.shape[2]...]
    dot_general x23 -> x0, matrix products: 26.9 us -> none  [the longest x5 18.8 us: add_block(): jnp.dot(member.T, term_rows.reshape(block_rows, -1), precision=lax.Precis...]
    gather x9 -> x0, local copies, waits for them, and re-layouts: 23.4 us -> none  [the longest x5 9.87 us: score_block(): jnp.take(ref_harm, pick_block, axis=0)]
    while x5 -> x0, local copies, waits for them, and re-layouts: 22.3 us -> none
    all_to_all x5 -> x0, starting transfers between devices: 20.6 us -> none  [the longest x1 5.27 us: on_device(): lax.all_to_all(payload, 'cls', split_axis=0, concat_axis=0, tiled=True)]
  transfers between devices with their start and end apart: 7 -> 0, of which waited for: 6 -> 0; matrix products, arithmetic and copies ran while one was open for 15% -> 0% of each run, Pallas kernels for 0% -> 0%
where the time goes in v2:
time: 71.5 us; the launch traced here: 70.5 us
  Pallas kernels  66.7 us (93%)
  local copies, waits for them, and re-layouts  3.09 us (4%)
    pallas_call x1, Pallas kernels, on_device(): pl.pallas_call(functools.partial(body, doms, owners, prior_count, deliver...  66.7 us
    unnamed x6, local copies, waits for them, and re-layouts  2.93 us

profile of v2, /device:TPU:0, one launch (start us, length us, event | category | flops | bytes accessed | tf_op | source)
XLA Modules:
  0.0 70.5 jit_solution(8442173749663735899)
XLA Ops:
  0.0 0.0 copy-start.1
  0.0 0.1 pad.2.clone
  0.1 0.6 copy-done.1
  0.7 0.0 copy-start
  0.7 0.1 copy.10
  0.7 0.6 copy-done
  1.3 0.1 copy.9
  1.4 0.7 add_add_fusion.meta_ref
  2.1 66.7 %shard_map.82 = f32[256,256]{1,0:T(8,128)} custom-call(bf16[32,64,256]{2,1,0:T(8,128)(2,1)} %img_ref.1, bf16[16,64,256]{2,1,0:T(8,128)(2,1)} %ref_ref.1, s32[32,128]{1,0:T(8,128)} %add_add_fusion.meta_ref, f32[64,64]{1,0:T(8,128)} %ctf_ref.1, bf16[256,256]{1,0:T(8,128)(2,1)} %constant.10.clone.swap_ref, f32[256,256]{1,0:T(8,128)} %constant.8.clone.forward_ref, ...), custom_call_target="tpu_custom_call" | custom-call | tf_op jit(solution)/shard_map/pallas_call | solution.py:331
  68.8 1.7 %copy.12 = f32[16,16,256]{2,1,0:T(8,128)} copy(f32[16,16,256]{2,1,0:T(8,128)} %bitcast.2) | data formatting | bytes 524288
  (1 shorter events, 0.0 us)
Async XLA Ops:
  0.0 0.7 copy-start.1
  0.7 0.7 copy-start

commit v3 on v2

v3 whole, which is shorter than its diff:
```python
import functools

import jax
import jax.numpy as jnp
import numpy as np
from jax import lax
from jax.experimental import pallas as pl
from jax.experimental.pallas import tpu as pltpu
from jax.sharding import PartitionSpec as P

MESH = pl.DeviceIdType.MESH
VMEM = pl.BlockSpec(memory_space=pltpu.VMEM)
LIMIT = 56 * 1024 * 1024
F32 = jnp.float32
BF16 = jnp.bfloat16
EXACT = lax.Precision.HIGHEST
TILE = 16
CORES = 2


def angle_tables(angles):
    harm_count = angles // 2
    phase = np.arange(angles)[:, None] * np.arange(harm_count)[None, :] % angles
    grid = 2.0 * np.pi / angles * phase
    cosine, sine = np.cos(grid), np.sin(grid)
    forward = np.concatenate([cosine, sine], axis=1)
    weight = np.where(np.arange(harm_count) == 0, 1.0, 2.0)[:, None] / angles
    inverse = np.concatenate([cosine.T * weight, -sine.T * weight], axis=0)
    return forward.astype(np.float32), inverse.astype(np.float32)


def swap_matrix():
    rows = np.arange(TILE * TILE)
    swap = np.zeros((TILE * TILE, TILE * TILE), np.float32)
    swap[rows, rows % TILE * TILE + rows // TILE] = 1.0
    return swap


def harmonics(src, dst, swap, table, place):
    frames, cycles, angles = src.shape
    for first in range(0, cycles, TILE):
        for frame in range(0, frames, TILE):
            block = src[frame : frame + TILE, first : first + TILE, :]
            block = block.reshape(TILE * TILE, angles)
            block = jnp.dot(swap, block, preferred_element_type=F32).astype(BF16)
            out = jnp.dot(block, table, preferred_element_type=F32).astype(BF16)
            for r in range(TILE):
                chip, s = place(first + r)
                dst[chip, s, frame : frame + TILE, :] = out[r * TILE : (r + 1) * TILE]


def column(rows, index):
    lanes = lax.broadcasted_iota(jnp.int32, rows.shape, 1)
    return jnp.sum(jnp.where(lanes == index, rows, 0.0), axis=1, keepdims=True)


def class_hits(meta, priors, classes):
    lanes = lax.broadcasted_iota(jnp.int32, (meta.shape[0], classes), 1)
    return jnp.concatenate(
        [(meta[:, j : j + 1] == lanes).astype(F32) for j in range(priors)], axis=0
    )


def ctf_rows(meta, priors, table):
    groups = table.shape[0]
    lanes = lax.broadcasted_iota(jnp.int32, (meta.shape[0], groups), 1)
    hits = (meta[:, priors : priors + 1] == lanes).astype(F32)
    return jnp.dot(hits, table, precision=EXACT, preferred_element_type=F32)


def body(
    doms,
    chips,
    priors,
    deliver,
    img_ref,
    ref_ref,
    meta_ref,
    ctf_ref,
    swap_ref,
    forward_ref,
    inverse_ref,
    *rest,
):
    if deliver:
        out_ref, rest = rest[0], rest[1:]
    else:
        sum_out, norm_out, rest = rest[0], rest[1], rest[2:]
    (
        part_send,
        part_got,
        cls_send,
        cls_got,
        meta_got,
        scaled,
        ctf_got,
        score_send,
        score_got,
        spec_send,
        spec_got,
        sums,
        norms,
        half_send,
        half_got,
        half_norm,
        half_norm_got,
        sum_send,
        sum_got,
        norm_send,
        norm_got,
        low,
        high,
        cls_sem,
        pass_sem,
        meta_sem,
        part_sem,
        score_sem,
        spec_sem,
        half_sem,
        sum_sem,
        norm_sem,
    ) = rest
    dom, me = lax.axis_index("dom"), lax.axis_index("cls")
    chip, core = me // CORES, me % CORES
    sibling = (dom, me + 1 - 2 * core)
    particles, cycles, angles = img_ref.shape
    owned = ref_ref.shape[0]
    owners = chips * CORES
    classes = owners * owned
    share = cycles // chips
    harm = angles // 2
    width = 2 * harm
    held = cycles // doms
    run = max(held // owners, 1)

    def place(r):
        if not deliver:
            return r // share, r % share
        to, chip, half, one = r // held, r % held // (CORES * run), r // run % CORES, r % run
        return chip, (half * doms + to) * run + one

    places = {place(r): r for r in range(cycles)}
    first_cycle = [places[0, s] for s in range(share)]
    chip_step = places[1, 0] - places[0, 0]

    barrier = pltpu.get_barrier_semaphore()
    offsets = [(a, b) for a in range(doms if deliver else 1) for b in range(owners)][1:]

    def peer(a, b):
        return (lax.rem(dom + a, doms), lax.rem(me + b, owners))

    def chip_at(off):
        return lax.rem(chip + off + chips, chips)

    def remote(src, dst, sem, at, device):
        return pltpu.make_async_remote_copy(
            src_ref=src,
            dst_ref=dst,
            send_sem=sem.at[(0,) + at],
            recv_sem=sem.at[(1,) + at],
            device_id=device,
            device_id_type=MESH,
        )

    def same_core(off):
        return (dom, chip_at(off) * CORES + core)

    def cls_copy(off):
        return remote(cls_send.at[chip_at(off)], cls_got.at[me], cls_sem, (off,), same_core(off))

    def pass_copy(off):
        slot = cls_got.at[chip_at(-off) * CORES + core]
        return remote(slot, slot, pass_sem, (off,), sibling)

    def pass_got(off):
        slot = cls_got.at[chip_at(-off) * CORES + 1 - core]
        return remote(slot, slot, pass_sem, (off,), sibling)

    def meta_copy(off):
        return remote(meta_ref, meta_got.at[chip], meta_sem, (off,), same_core(off))

    def part_copy(off):
        return remote(
            part_send.at[chip_at(off)], part_got.at[chip], part_sem, (off,), same_core(off)
        )

    def score_copy(off):
        return remote(
            score_send.at[chip_at(-off)], score_got.at[chip], score_sem, (off,), same_core(-off)
        )

    def spec_copy(off):
        return remote(spec_send, spec_got.at[chip], spec_sem, (off,), same_core(off))

    for a, b in offsets:
        pl.semaphore_signal(barrier, inc=1, device_id=peer(a, b), device_id_type=MESH)
    table = forward_ref[...].astype(BF16)
    swap = swap_ref[...]
    harmonics(ref_ref, cls_send, swap, table, place)
    cls_got[me] = cls_send[chip]
    pl.semaphore_wait(barrier, len(offsets))
    for off in range(1, chips):
        meta_copy(off).start()
        cls_copy(off).start()
    pass_copy(0).start()
    harmonics(img_ref, part_send, swap, table, place)
    for off in range(1, chips):
        part_copy(off).start()
    part_got[chip] = part_send[chip]
    meta_got[chip] = meta_ref[...]

    def score(src):
        meta = meta_got[src]
        ctf = ctf_rows(meta, priors, ctf_ref[...])
        ctf_got[src] = ctf
        hits = class_hits(meta, priors, classes).astype(BF16)
        real, imag = 0.0, 0.0
        for s in range(share):
            part = part_got[src, s].astype(F32) * column(ctf, first_cycle[s] + chip_step * chip)
            scaled[src, s] = part
            table = cls_got[:, s].reshape(classes, width)
            picked = jnp.dot(hits, table, preferred_element_type=F32)
            picked = picked.reshape(priors, particles, width)
            pc, ps = part[None, :, :harm], part[None, :, harm:]
            cc, cs = picked[:, :, :harm], picked[:, :, harm:]
            real = real + (pc * cc + ps * cs)
            imag = imag + (pc * cs - ps * cc)
        score_send[src, :, :, :harm] = real.astype(BF16)
        score_send[src, :, :, harm:] = imag.astype(BF16)

    for off in range(1, chips):
        meta_copy(off).wait()
        cls_copy(off).wait()
        pass_copy(off).start()
    for off in range(chips):
        pass_copy(off).wait_send()
        pass_got(off).wait_recv()

    score(chip)

    @pl.loop(1, chips)
    def _(off):
        part_copy(off).wait_recv()
        score(chip_at(-off))
        score_copy(off).start()

    joined = score_send[chip].astype(F32)
    for off in range(1, chips):
        score_copy(off).wait_recv()
        joined = joined + score_got[chip_at(off)].astype(F32)
    joined = joined.reshape(priors * particles, width)
    scores = jnp.dot(joined, inverse_ref[...], precision=EXACT, preferred_element_type=F32)
    scores = scores.reshape(priors, particles, angles)
    highest = jnp.max(jnp.max(scores, axis=0), axis=1, keepdims=True)
    total = jnp.sum(jnp.sum(jnp.exp(scores - highest[None]), axis=0), axis=1, keepdims=True)
    log_total = highest + jnp.log(total)
    weights = jnp.exp(scores - log_total[None]).reshape(priors * particles, angles)
    spectrum = jnp.dot(weights, forward_ref[...], precision=EXACT, preferred_element_type=F32)
    spec_send[...] = spectrum.astype(BF16).reshape(spec_send.shape)
    for off in range(1, chips):
        spec_copy(off).start()
    spec_got[chip] = spec_send[...]
    sums[...] = jnp.zeros_like(sums)
    norms[...] = jnp.zeros_like(norms)

    def add(src):
        hits = class_hits(meta_got[src], priors, classes).T
        spectrum = spec_got[src].astype(F32)
        wc, ws = spectrum[:, :, :harm], spectrum[:, :, harm:]
        ctf = ctf_got[src]
        square = (ctf * ctf)[None] * wc[:, :, :1]
        norms[...] += jnp.dot(
            hits,
            square.reshape(priors * particles, cycles),
            precision=EXACT,
            preferred_element_type=F32,
        )
        hits = hits.astype(BF16)
        for s in range(share):
            part = scaled[src, s][None]
            pc, ps = part[:, :, :harm], part[:, :, harm:]
            terms = jnp.concatenate([pc * wc + ps * ws, ps * wc - pc * ws], axis=2)
            terms = terms.reshape(priors * particles, width).astype(BF16)
            sums[s] += jnp.dot(hits, terms, preferred_element_type=F32)

    add(chip)

    @pl.loop(1, chips)
    def _(off):
        spec_copy(off).wait_recv()
        add(chip_at(-off))

    for off in range(1, chips):
        part_copy(off).wait_send()
        score_copy(off).wait_send()
        spec_copy(off).wait_send()

    if not deliver:
        sum_out[...] = sums[...].astype(BF16)
        norm_out[...] = norms[...]
        return

    half = doms * run
    mine = pl.multiple_of(me * owned, owned)
    other = pl.multiple_of(sibling[1] * owned, owned)
    half_send[...] = sums[pl.ds((1 - core) * half, half)].astype(BF16)
    half_norm[:, :cycles] = norms[pl.ds(other, owned), :]
    sum_half = remote(half_send, half_got, half_sem, (0,), sibling)
    norm_half = remote(half_norm, half_norm_got, half_sem, (1,), sibling)
    sum_half.start()
    norm_half.start()
    sum_half.wait()
    norm_half.wait()
    norm_send[:, :cycles] = norms[pl.ds(mine, owned), :] + half_norm_got[:, :cycles]

    def sum_copy(a, b):
        to = peer(a, b)
        start = pl.multiple_of(to[1] * owned, owned)
        src = sum_send.at[pl.ds(to[0] * run, run), pl.ds(start, owned), :]
        return remote(src, sum_got.at[dom, me], sum_sem, (a, b), to)

    def norm_copy(a):
        return remote(norm_send, norm_got.at[dom], norm_sem, (a,), peer(a, 0))

    for a in sorted(range(doms), key=lambda a: (a == 0, abs(a - doms // 2))):
        at = pl.ds(peer(a, 0)[0] * run, run)
        own = sums[pl.ds(core * half + peer(a, 0)[0] * run, run)]
        sum_send[at] = (own + half_got[at].astype(F32)).astype(BF16)
        for b in range(owners):
            if (a, b) in offsets:
                sum_copy(a, b).start()
        if a:
            norm_copy(a).start()
    sum_got[dom, me] = sum_send[pl.ds(dom * run, run), pl.ds(mine, owned), :]
    norm_got[dom] = norm_send[...]
    for a, b in offsets:
        sum_copy(a, b).wait()
    for a in range(1, doms):
        norm_copy(a).wait()
    total_norm = norm_got[0, :, :cycles]
    for a in range(1, doms):
        total_norm = total_norm + norm_got[a, :, :cycles]
    for c in range(owners):
        for one in range(run):
            cycle = c * run + one
            result = sum_got[0, c, one].astype(F32)
            for a in range(1, doms):
                result = result + sum_got[a, c, one].astype(F32)
            result = result / (column(total_norm, dom * held + cycle) + 1.0)
            at = pl.ds(cycle, owned, stride=held)
            low[at, :] = result[:, :harm]
            high[at, :] = result[:, harm:]
    out_ref[:, :harm] = low[...]
    out_ref[:, harm:] = high[...]


def on_device(doms, images, references, ctf_table, defocus, priors):
    owners = lax.axis_size("cls")
    particles, cycles, angles = images.shape
    owned = references.shape[0]
    classes = owners * owned
    prior_count = priors.shape[1]
    chips = owners // CORES
    share = cycles // chips
    width = angles // 2 * 2
    held = cycles // doms
    deliver = held % owners == 0
    run = max(held // owners, 1)
    forward, inverse = (jnp.asarray(t) for t in angle_tables(angles))
    swap = jnp.asarray(swap_matrix(), BF16)
    meta = jnp.concatenate(
        [priors, defocus[:, None], jnp.zeros((particles, 127 - prior_count), jnp.int32)], axis=1
    )
    if deliver:
        shapes = [jax.ShapeDtypeStruct((owned * held, width), F32)]
    else:
        shapes = [
            jax.ShapeDtypeStruct((share, classes, width), BF16),
            jax.ShapeDtypeStruct((classes, cycles), F32),
        ]
    slots = (prior_count, particles, width)
    sums = (share, classes, width)
    half = (doms * run, classes, width)
    pair_sem = pltpu.SemaphoreType.DMA((2, chips))
    done = pl.pallas_call(
        functools.partial(body, doms, chips, prior_count, deliver),
        out_shape=shapes,
        in_specs=[VMEM] * 7,
        out_specs=[VMEM] * len(shapes),
        scratch_shapes=[
            pltpu.VMEM((chips, share, particles, width), BF16),
            pltpu.VMEM((chips, share, particles, width), BF16),
            pltpu.VMEM((chips, share, owned, width), BF16),
            pltpu.VMEM((owners, share, owned, width), BF16),
            pltpu.VMEM((chips,) + meta.shape, jnp.int32),
            pltpu.VMEM((chips, share, particles, width), F32),
            pltpu.VMEM((chips, particles, cycles), F32),
            pltpu.VMEM((chips,) + slots, BF16),
            pltpu.VMEM((chips,) + slots, BF16),
            pltpu.VMEM(slots, BF16),
            pltpu.VMEM((chips,) + slots, BF16),
            pltpu.VMEM(sums, F32),
            pltpu.VMEM((classes, cycles), F32),
            pltpu.VMEM(half, BF16),
            pltpu.VMEM(half, BF16),
            pltpu.VMEM((owned, 128), F32),
            pltpu.VMEM((owned, 128), F32),
            pltpu.VMEM(half, BF16),
            pltpu.VMEM((doms, owners, run, owned, width), BF16),
            pltpu.VMEM((owned, 128), F32),
            pltpu.VMEM((doms, owned, 128), F32),
            pltpu.VMEM((owned * held, width // 2), F32),
            pltpu.VMEM((owned * held, width // 2), F32),
            pair_sem,
            pair_sem,
            pair_sem,
            pair_sem,
            pair_sem,
            pair_sem,
            pltpu.SemaphoreType.DMA((2, 2)),
            pltpu.SemaphoreType.DMA((2, doms, owners)),
            pltpu.SemaphoreType.DMA((2, doms)),
        ],
        compiler_params=pltpu.CompilerParams(
            collective_id=1, has_side_effects=True, vmem_limit_bytes=LIMIT
        ),
    )(images, references, meta, ctf_table, swap, forward, inverse)
    if deliver:
        return done[0].reshape(owned, held, width)
    sums, norms = done
    me = lax.axis_index("cls")
    chip, core = me // CORES, me % CORES
    mine = chip * share + jnp.arange(share)
    placed = jnp.zeros((cycles, classes, width), F32).at[mine].set(sums.astype(F32))
    placed = lax.psum_scatter(placed, "dom", scatter_dimension=0, tiled=True)
    placed = lax.psum_scatter(placed, "cls", scatter_dimension=1, tiled=True)
    rows = jnp.arange(classes)[:, None] // (CORES * owned)
    norms = jnp.where(rows == chip, norms, 0.0)
    norms = lax.psum_scatter(norms, "dom", scatter_dimension=1, tiled=True)
    norms = lax.psum_scatter(norms, "cls", scatter_dimension=0, tiled=True)
    return placed.transpose(1, 0, 2) / (norms + 1.0)[:, :, None]


def solution(mesh):
    return jax.shard_map(
        functools.partial(on_device, mesh.shape["dom"]),
        mesh=mesh,
        in_specs=(
            P(("dom", "cls"), None, None),
            P("cls", None, None),
            P(),
            P(("dom", "cls")),
            P(("dom", "cls"), None),
        ),
        out_specs=P("cls", "dom", None),
        check_vma=False,
    )
```

time: 71.5 us -> 66 us (0.923)
  Pallas kernels: 66.7 us -> 61.1 us
    pallas_call x1, Pallas kernels: 66.7 us -> 61.1 us  [on_device(): pl.pallas_call(functools.partial(body, doms, chips, prior_count, deliver)...]
where the time goes in v3:
time: 66 us; the launch traced here: 64.9 us
  Pallas kernels  61.1 us (93%)
  local copies, waits for them, and re-layouts  3.09 us (5%)
  other arithmetic  0.68 us (1%)
    pallas_call x1, Pallas kernels, on_device(): pl.pallas_call(functools.partial(body, doms, chips, prior_count, deliver)...  61.1 us
    unnamed x6, local copies, waits for them, and re-layouts  2.93 us

profile of v3, /device:TPU:0, one launch (start us, length us, event | category | flops | bytes accessed | tf_op | source)
XLA Modules:
  0.0 64.9 jit_solution(14861095788029682361)
XLA Ops:
  0.0 0.0 copy-start.1
  0.0 0.1 pad.2.clone
  0.1 0.6 copy-done.1
  0.7 0.0 copy-start
  0.7 0.1 copy.10
  0.7 0.6 copy-done
  1.3 0.1 copy.9
  1.4 0.7 %add_add_fusion.meta_ref = s32[32,128]{1,0:T(8,128)} fusion(s32[32,1]{1,0:T(8,128)S(1)} %copy.10, s32[32,8]{1,0:T(8,128)S(1)} %copy.9, s32[128]{0:T(128)S(1)} %pad.2.clone), kind=kLoop, calls=%fused_computation | loop fusion | flops 8192 | bytes 18048 | tf_op jit(solution)/shard_map/concatenate | solution.py:371
  2.1 61.1 %shard_map.82 = f32[256,256]{1,0:T(8,128)} custom-call(bf16[32,64,256]{2,1,0:T(8,128)(2,1)} %img_ref.1, bf16[16,64,256]{2,1,0:T(8,128)(2,1)} %ref_ref.1, s32[32,128]{1,0:T(8,128)} %add_add_fusion.meta_ref, f32[64,64]{1,0:T(8,128)} %ctf_ref.1, bf16[256,256]{1,0:T(8,128)(2,1)} %constant.10.clone.swap_ref, f32[256,256]{1,0:T(8,128)} %constant.8.clone.forward_ref, ...), custom_call_target="tpu_custom_call" | custom-call | tf_op jit(solution)/shard_map/pallas_call | solution.py:385
  63.2 1.7 %copy.12 = f32[16,16,256]{2,1,0:T(8,128)} copy(f32[16,16,256]{2,1,0:T(8,128)} %bitcast.2) | data formatting | bytes 524288
  (1 shorter events, 0.0 us)
Async XLA Ops:
  0.0 0.7 %copy-start.1 = (s32[32]{0:T(128)S(1)}, s32[32]{0:T(128)}, u32[]{:S(2)}) copy-start(s32[32]{0:T(128)} %param.11) | copy-start | bytes 388
  0.7 0.7 %copy-start = (s32[32,8]{0,1:T(8,128)S(1)}, s32[32,8]{0,1:T(8,128)}, u32[]{:S(2)}) copy-start(s32[32,8]{0,1:T(8,128)} %param.12) | copy-start | bytes 3076

commit v4 on v3

--- a/solution.py
+++ b/solution.py
@@ -16,6 +16,7 @@
 EXACT = lax.Precision.HIGHEST
 TILE = 16
 CORES = 2
+BATCHES = 2
 
 
 def angle_tables(angles):
@@ -59,6 +60,19 @@
     return jnp.concatenate(
         [(meta[:, j : j + 1] == lanes).astype(F32) for j in range(priors)], axis=0
     )
+
+
+def split(rows):
+    high = rows.astype(BF16)
+    return high, (rows - high.astype(F32)).astype(BF16)
+
+
+def table_product(rows, table):
+    high, low = split(rows)
+    table_high, table_low = split(table)
+    total = jnp.dot(high, table_low, preferred_element_type=F32)
+    total = total + jnp.dot(low, table_high, preferred_element_type=F32)
+    return total + jnp.dot(high, table_high, preferred_element_type=F32)
 
 
 def ctf_rows(meta, priors, table):
@@ -87,6 +101,7 @@
     else:
         sum_out, norm_out, rest = rest[0], rest[1], rest[2:]
     (
+        img_got,
         part_send,
         part_got,
         cls_send,
@@ -94,6 +109,9 @@
         meta_got,
         scaled,
         ctf_got,
+        hits,
+        hits_t,
+        terms,
         score_send,
         score_got,
         spec_send,
@@ -110,6 +128,7 @@
         norm_got,
         low,
         high,
+        img_sem,
         cls_sem,
         pass_sem,
         meta_sem,
@@ -124,6 +143,8 @@
     chip, core = me // CORES, me % CORES
     sibling = (dom, me + 1 - 2 * core)
     particles, cycles, angles = img_ref.shape
+    batch = particles // BATCHES
+    slots = priors * batch
     owned = ref_ref.shape[0]
     owners = chips * CORES
     classes = owners * owned
@@ -179,19 +200,32 @@
     def meta_copy(off):
         return remote(meta_ref, meta_got.at[chip], meta_sem, (off,), same_core(off))
 
-    def part_copy(off):
+    def frames_of(b):
+        return pl.ds(b * batch, batch)
+
+    def part_copy(off, b):
         return remote(
-            part_send.at[chip_at(off)], part_got.at[chip], part_sem, (off,), same_core(off)
+            part_send.at[chip_at(off), :, frames_of(b), :],
+            part_got.at[chip, :, frames_of(b), :],
+            part_sem,
+            (off, b),
+            same_core(off),
         )
 
-    def score_copy(off):
+    def score_copy(off, b):
         return remote(
-            score_send.at[chip_at(-off)], score_got.at[chip], score_sem, (off,), same_core(-off)
+            score_send.at[chip_at(-off), b],
+            score_got.at[chip, b],
+            score_sem,
+            (off, b),
+            same_core(-off),
         )
 
-    def spec_copy(off):
-        return remote(spec_send, spec_got.at[chip], spec_sem, (off,), same_core(off))
-
+    def spec_copy(off, b):
+        return remote(spec_send.at[b], spec_got.at[chip, b], spec_sem, (off, b), same_core(off))
+
+    images = pltpu.make_async_copy(img_ref, img_got, img_sem)
+    images.start()
     for a, b in offsets:
         pl.semaphore_signal(barrier, inc=1, device_id=peer(a, b), device_id_type=MESH)
     table = forward_ref[...].astype(BF16)
@@ -203,116 +237,131 @@
         meta_copy(off).start()
         cls_copy(off).start()
     pass_copy(0).start()
-    harmonics(img_ref, part_send, swap, table, place)
-    for off in range(1, chips):
-        part_copy(off).start()
+    images.wait()
+    harmonics(img_got, part_send, swap, table, place)
+    for b in range(BATCHES):
+        for off in range(1, chips):
+            part_copy(off, b).start()
     part_got[chip] = part_send[chip]
     meta_got[chip] = meta_ref[...]
-
-    def score(src):
-        meta = meta_got[src]
-        ctf = ctf_rows(meta, priors, ctf_ref[...])
-        ctf_got[src] = ctf
-        hits = class_hits(meta, priors, classes).astype(BF16)
-        real, imag = 0.0, 0.0
-        for s in range(share):
-            part = part_got[src, s].astype(F32) * column(ctf, first_cycle[s] + chip_step * chip)
-            scaled[src, s] = part
-            table = cls_got[:, s].reshape(classes, width)
-            picked = jnp.dot(hits, table, preferred_element_type=F32)
-            picked = picked.reshape(priors, particles, width)
-            pc, ps = part[None, :, :harm], part[None, :, harm:]
-            cc, cs = picked[:, :, :harm], picked[:, :, harm:]
-            real = real + (pc * cc + ps * cs)
-            imag = imag + (pc * cs - ps * cc)
-        score_send[src, :, :, :harm] = real.astype(BF16)
-        score_send[src, :, :, harm:] = imag.astype(BF16)
-
+    sums[...] = jnp.zeros_like(sums)
+    norms[...] = jnp.zeros_like(norms)
     for off in range(1, chips):
         meta_copy(off).wait()
+
+    def lanes_of(src, b):
+        return pl.ds(pl.multiple_of((src * BATCHES + b) * slots, slots), slots)
+
+    @pl.loop(0, chips)
+    def _(src):
+        ctf_got[src] = ctf_rows(meta_got[src], priors, ctf_ref[...])
+        for b in range(BATCHES):
+            found = class_hits(meta_got[src, frames_of(b)], priors, classes)
+            hits[src, b] = found.astype(BF16)
+            hits_t[:, lanes_of(src, b)] = found.T.astype(BF16)
+
+    for off in range(1, chips):
         cls_copy(off).wait()
         pass_copy(off).start()
     for off in range(chips):
         pass_copy(off).wait_send()
         pass_got(off).wait_recv()
 
-    score(chip)
-
-    @pl.loop(1, chips)
-    def _(off):
-        part_copy(off).wait_recv()
-        score(chip_at(-off))
-        score_copy(off).start()
-
-    joined = score_send[chip].astype(F32)
-    for off in range(1, chips):
-        score_copy(off).wait_recv()
-        joined = joined + score_got[chip_at(off)].astype(F32)
-    joined = joined.reshape(priors * particles, width)
-    scores = jnp.dot(joined, inverse_ref[...], precision=EXACT, preferred_element_type=F32)
-    scores = scores.reshape(priors, particles, angles)
-    highest = jnp.max(jnp.max(scores, axis=0), axis=1, keepdims=True)
-    total = jnp.sum(jnp.sum(jnp.exp(scores - highest[None]), axis=0), axis=1, keepdims=True)
-    log_total = highest + jnp.log(total)
-    weights = jnp.exp(scores - log_total[None]).reshape(priors * particles, angles)
-    spectrum = jnp.dot(weights, forward_ref[...], precision=EXACT, preferred_element_type=F32)
-    spec_send[...] = spectrum.astype(BF16).reshape(spec_send.shape)
-    for off in range(1, chips):
-        spec_copy(off).start()
-    spec_got[chip] = spec_send[...]
-    sums[...] = jnp.zeros_like(sums)
-    norms[...] = jnp.zeros_like(norms)
-
-    def add(src):
-        hits = class_hits(meta_got[src], priors, classes).T
-        spectrum = spec_got[src].astype(F32)
+    def score(src, b):
+        ctf = ctf_got[src, frames_of(b)]
+        real, imag = 0.0, 0.0
+        for s in range(share):
+            part = part_got[src, s, frames_of(b)].astype(F32)
+            part = part * column(ctf, first_cycle[s] + chip_step * chip)
+            scaled[src, s, frames_of(b)] = part
+            table = cls_got[:, s].reshape(classes, width)
+            picked = jnp.dot(hits[src, b], table, preferred_element_type=F32)
+            picked = picked.reshape(priors, batch, width)
+            pc, ps = part[None, :, :harm], part[None, :, harm:]
+            cc, cs = picked[:, :, :harm], picked[:, :, harm:]
+            real = real + (pc * cc + ps * cs)
+            imag = imag + (pc * cs - ps * cc)
+        score_send[src, b, :, :, :harm] = real.astype(BF16)
+        score_send[src, b, :, :, harm:] = imag.astype(BF16)
+
+    for b in range(BATCHES):
+        score(chip, b)
+    for b in range(BATCHES):
+
+        @pl.loop(1, chips)
+        def _(off):
+            part_copy(off, b).wait_recv()
+            score(chip_at(-off), b)
+            score_copy(off, b).start()
+
+    for b in range(BATCHES):
+        joined = score_send[chip, b].astype(F32)
+        for off in range(1, chips):
+            score_copy(off, b).wait_recv()
+            joined = joined + score_got[chip_at(off), b].astype(F32)
+        scores = table_product(joined.reshape(slots, width), inverse_ref[...])
+        scores = scores.reshape(priors, batch, angles)
+        highest = jnp.max(jnp.max(scores, axis=0), axis=1, keepdims=True)
+        total = jnp.sum(jnp.exp(scores - highest[None]), axis=0)
+        log_total = highest + jnp.log(jnp.sum(total, axis=1, keepdims=True))
+        weights = jnp.exp(scores - log_total[None]).reshape(slots, angles)
+        spectrum = table_product(weights, forward_ref[...])
+        spec_send[b] = spectrum.astype(BF16).reshape(priors, batch, width)
+        for off in range(1, chips):
+            spec_copy(off, b).start()
+        spec_got[chip, b] = spec_send[b]
+
+    half = doms * run
+    other_half, own_half = ((1 - core) * half, core * half) if deliver else (0, 0)
+
+    def slot_terms(src, b, s):
+        spectrum = spec_got[src, b].astype(F32)
         wc, ws = spectrum[:, :, :harm], spectrum[:, :, harm:]
-        ctf = ctf_got[src]
-        square = (ctf * ctf)[None] * wc[:, :, :1]
-        norms[...] += jnp.dot(
-            hits,
-            square.reshape(priors * particles, cycles),
-            precision=EXACT,
-            preferred_element_type=F32,
-        )
-        hits = hits.astype(BF16)
-        for s in range(share):
-            part = scaled[src, s][None]
-            pc, ps = part[:, :, :harm], part[:, :, harm:]
-            terms = jnp.concatenate([pc * wc + ps * ws, ps * wc - pc * ws], axis=2)
-            terms = terms.reshape(priors * particles, width).astype(BF16)
-            sums[s] += jnp.dot(hits, terms, preferred_element_type=F32)
-
-    add(chip)
-
-    @pl.loop(1, chips)
-    def _(off):
-        spec_copy(off).wait_recv()
-        add(chip_at(-off))
-
-    for off in range(1, chips):
-        part_copy(off).wait_send()
-        score_copy(off).wait_send()
-        spec_copy(off).wait_send()
+        part = scaled[src, s, frames_of(b)][None]
+        pc, ps = part[:, :, :harm], part[:, :, harm:]
+        both = jnp.concatenate([pc * wc + ps * ws, ps * wc - pc * ws], axis=2)
+        return both.reshape(slots, width).astype(BF16)
+
+    def add(src, b):
+        chosen = hits_t[:, lanes_of(src, b)]
+        ctf = ctf_got[src, frames_of(b)]
+        square = (ctf * ctf)[None] * spec_got[src, b, :, :, :1].astype(F32)
+        parts = jnp.concatenate(split(square.reshape(slots, cycles)), axis=1)
+        norms[...] += jnp.dot(chosen, parts, preferred_element_type=F32)
+        for i in range(sums.shape[0]):
+            sums[i] += jnp.dot(
+                chosen, slot_terms(src, b, other_half + i), preferred_element_type=F32
+            )
+
+    for b in range(BATCHES):
+        add(chip, b)
+    for b in range(BATCHES):
+
+        @pl.loop(1, chips)
+        def _(off):
+            spec_copy(off, b).wait_recv()
+            add(chip_at(-off), b)
+
+    for b in range(BATCHES):
+        for off in range(1, chips):
+            part_copy(off, b).wait_send()
+            score_copy(off, b).wait_send()
+            spec_copy(off, b).wait_send()
+    norms[:, :cycles] += norms[:, cycles:]
 
     if not deliver:
         sum_out[...] = sums[...].astype(BF16)
-        norm_out[...] = norms[...]
+        norm_out[...] = norms[:, :cycles]
         return
 
-    half = doms * run
     mine = pl.multiple_of(me * owned, owned)
     other = pl.multiple_of(sibling[1] * owned, owned)
-    half_send[...] = sums[pl.ds((1 - core) * half, half)].astype(BF16)
-    half_norm[:, :cycles] = norms[pl.ds(other, owned), :]
+    half_send[...] = sums[...].astype(BF16)
+    half_norm[...] = norms[pl.ds(other, owned), :]
     sum_half = remote(half_send, half_got, half_sem, (0,), sibling)
     norm_half = remote(half_norm, half_norm_got, half_sem, (1,), sibling)
     sum_half.start()
     norm_half.start()
-    sum_half.wait()
-    norm_half.wait()
-    norm_send[:, :cycles] = norms[pl.ds(mine, owned), :] + half_norm_got[:, :cycles]
-
     def sum_copy(a, b):
         to = peer(a, b)
         start = pl.multiple_of(to[1] * owned, owned)
@@ -322,10 +371,24 @@
     def norm_copy(a):
         return remote(norm_send, norm_got.at[dom], norm_sem, (a,), peer(a, 0))
 
+    waited = False
     for a in sorted(range(doms), key=lambda a: (a == 0, abs(a - doms // 2))):
-        at = pl.ds(peer(a, 0)[0] * run, run)
-        own = sums[pl.ds(core * half + peer(a, 0)[0] * run, run)]
-        sum_send[at] = (own + half_got[at].astype(F32)).astype(BF16)
+        first = peer(a, 0)[0] * run
+        own = []
+        for one in range(run):
+            for src in range(chips):
+                for b in range(BATCHES):
+                    at = pl.ds((src * BATCHES + b) * slots, slots)
+                    terms[one, at, :] = slot_terms(src, b, own_half + first + one)
+            own.append(jnp.dot(hits_t[...], terms[one], preferred_element_type=F32))
+        if not waited:
+            sum_half.wait()
+            norm_half.wait()
+            norm_send[...] = norms[pl.ds(mine, owned), :] + half_norm_got[...]
+            waited = True
+        for one in range(run):
+            both = own[one] + half_got[first + one].astype(F32)
+            sum_send[first + one] = both.astype(BF16)
         for b in range(owners):
             if (a, b) in offsets:
                 sum_copy(a, b).start()
@@ -378,16 +441,20 @@
             jax.ShapeDtypeStruct((share, classes, width), BF16),
             jax.ShapeDtypeStruct((classes, cycles), F32),
         ]
-    slots = (prior_count, particles, width)
+    batch = particles // BATCHES
+    slots = (BATCHES, prior_count, batch, width)
+    rows = prior_count * batch
     sums = (share, classes, width)
     half = (doms * run, classes, width)
     pair_sem = pltpu.SemaphoreType.DMA((2, chips))
+    batch_sem = pltpu.SemaphoreType.DMA((2, chips, BATCHES))
     done = pl.pallas_call(
         functools.partial(body, doms, chips, prior_count, deliver),
         out_shape=shapes,
-        in_specs=[VMEM] * 7,
+        in_specs=[pl.BlockSpec(memory_space=pl.ANY)] + [VMEM] * 6,
         out_specs=[VMEM] * len(shapes),
         scratch_shapes=[
+            pltpu.VMEM(images.shape, BF16),
             pltpu.VMEM((chips, share, particles, width), BF16),
             pltpu.VMEM((chips, share, particles, width), BF16),
             pltpu.VMEM((chips, share, owned, width), BF16),
@@ -395,28 +462,32 @@
             pltpu.VMEM((chips,) + meta.shape, jnp.int32),
             pltpu.VMEM((chips, share, particles, width), F32),
             pltpu.VMEM((chips, particles, cycles), F32),
+            pltpu.VMEM((chips, BATCHES, rows, classes), BF16),
+            pltpu.VMEM((classes, chips * BATCHES * rows), BF16),
+            pltpu.VMEM((run, chips * BATCHES * rows, width), BF16),
             pltpu.VMEM((chips,) + slots, BF16),
             pltpu.VMEM((chips,) + slots, BF16),
             pltpu.VMEM(slots, BF16),
             pltpu.VMEM((chips,) + slots, BF16),
-            pltpu.VMEM(sums, F32),
-            pltpu.VMEM((classes, cycles), F32),
+            pltpu.VMEM(half if deliver else sums, F32),
+            pltpu.VMEM((classes, 2 * cycles), F32),
             pltpu.VMEM(half, BF16),
             pltpu.VMEM(half, BF16),
-            pltpu.VMEM((owned, 128), F32),
-            pltpu.VMEM((owned, 128), F32),
+            pltpu.VMEM((owned, 2 * cycles), F32),
+            pltpu.VMEM((owned, 2 * cycles), F32),
             pltpu.VMEM(half, BF16),
             pltpu.VMEM((doms, owners, run, owned, width), BF16),
-            pltpu.VMEM((owned, 128), F32),
-            pltpu.VMEM((doms, owned, 128), F32),
+            pltpu.VMEM((owned, 2 * cycles), F32),
+            pltpu.VMEM((doms, owned, 2 * cycles), F32),
             pltpu.VMEM((owned * held, width // 2), F32),
             pltpu.VMEM((owned * held, width // 2), F32),
+            pltpu.SemaphoreType.DMA,
             pair_sem,
             pair_sem,
             pair_sem,
-            pair_sem,
-            pair_sem,
-            pair_sem,
+            batch_sem,
+            batch_sem,
+            batch_sem,
             pltpu.SemaphoreType.DMA((2, 2)),
             pltpu.SemaphoreType.DMA((2, doms, owners)),
             pltpu.SemaphoreType.DMA((2, doms)),
@@ -429,7 +500,7 @@
         return done[0].reshape(owned, held, width)
     sums, norms = done
     me = lax.axis_index("cls")
-    chip, core = me // CORES, me % CORES
+    chip = me // CORES
     mine = chip * share + jnp.arange(share)
     placed = jnp.zeros((cycles, classes, width), F32).at[mine].set(sums.astype(F32))
     placed = lax.psum_scatter(placed, "dom", scatter_dimension=0, tiled=True)

time: 66 us -> 59.9 us (0.908); the launches traced: 64.9 us -> 59.5 us
  Pallas kernels: 61.1 us -> 55.8 us
    pallas_call x1, Pallas kernels: 61.1 us -> 55.8 us  [on_device(): pl.pallas_call(functools.partial(body, doms, chips, prior_count, deliver)...]
where the time goes in v4:
time: 59.9 us; the launch traced here: 59.5 us
  Pallas kernels  55.8 us (93%)
  local copies, waits for them, and re-layouts  3.09 us (5%)
  other arithmetic  0.68 us (1%)
    pallas_call x1, Pallas kernels, on_device(): pl.pallas_call(functools.partial(body, doms, chips, prior_count, deliver)...  55.8 us
    unnamed x6, local copies, waits for them, and re-layouts  2.93 us

profile of v4, /device:TPU:0, one launch (start us, length us, event | category | flops | bytes accessed | tf_op | source)
XLA Modules:
  0.0 59.5 jit_solution(13569997464863064556)
XLA Ops:
  0.0 0.0 copy-start.1
  0.0 0.1 pad.2.clone
  0.1 0.6 copy-done.1
  0.7 0.0 copy-start
  0.7 0.1 copy.10
  0.7 0.6 %copy-done = s32[32,8]{0,1:T(8,128)S(1)} copy-done((s32[32,8]{0,1:T(8,128)S(1)}, s32[32,8]{0,1:T(8,128)}, u32[]{:S(2)}) %copy-start) | copy-done | bytes 1048
  1.3 0.1 copy.9
  1.4 0.7 %add_add_fusion.meta_ref = s32[32,128]{1,0:T(8,128)} fusion(s32[32,1]{1,0:T(8,128)S(1)} %copy.10, s32[32,8]{1,0:T(8,128)S(1)} %copy.9, s32[128]{0:T(128)S(1)} %pad.2.clone), kind=kLoop, calls=%fused_computation | loop fusion | flops 8192 | bytes 18048 | tf_op jit(solution)/shard_map/concatenate | solution.py:434
  2.1 55.8 %shard_map.82 = f32[256,256]{1,0:T(8,128)} custom-call(bf16[32,64,256]{2,1,0:T(8,128)(2,1)} %img_ref.1, bf16[16,64,256]{2,1,0:T(8,128)(2,1)} %ref_ref.1, s32[32,128]{1,0:T(8,128)} %add_add_fusion.meta_ref, f32[64,64]{1,0:T(8,128)} %ctf_ref.1, bf16[256,256]{1,0:T(8,128)(2,1)} %constant.10.clone.swap_ref, f32[256,256]{1,0:T(8,128)} %constant.8.clone.forward_ref, ...), custom_call_target="tpu_custom_call" | custom-call | tf_op jit(solution)/shard_map/pallas_call | solution.py:451
  57.9 1.7 %copy.12 = f32[16,16,256]{2,1,0:T(8,128)} copy(f32[16,16,256]{2,1,0:T(8,128)} %bitcast.2) | data formatting | bytes 524288
  (1 shorter events, 0.0 us)
Async XLA Ops:
  0.0 0.7 %copy-start.1 = (s32[32]{0:T(128)S(1)}, s32[32]{0:T(128)}, u32[]{:S(2)}) copy-start(s32[32]{0:T(128)} %param.11) | copy-start | bytes 388
  0.7 0.7 %copy-start = (s32[32,8]{0,1:T(8,128)S(1)}, s32[32,8]{0,1:T(8,128)}, u32[]{:S(2)}) copy-start(s32[32,8]{0,1:T(8,128)} %param.12) | copy-start | bytes 3076

commit v5 on v4

--- a/solution.py
+++ b/solution.py
@@ -89,7 +89,8 @@
     deliver,
     img_ref,
     ref_ref,
-    meta_ref,
+    priors_ref,
+    defocus_ref,
     ctf_ref,
     swap_ref,
     forward_ref,
@@ -97,7 +98,7 @@
     *rest,
 ):
     if deliver:
-        out_ref, rest = rest[0], rest[1:]
+        sum_got, norm_got, rest = rest[0], rest[1], rest[2:]
     else:
         sum_out, norm_out, rest = rest[0], rest[1], rest[2:]
     (
@@ -106,6 +107,7 @@
         part_got,
         cls_send,
         cls_got,
+        meta_send,
         meta_got,
         scaled,
         ctf_got,
@@ -123,11 +125,7 @@
         half_norm,
         half_norm_got,
         sum_send,
-        sum_got,
         norm_send,
-        norm_got,
-        low,
-        high,
         img_sem,
         cls_sem,
         pass_sem,
@@ -198,7 +196,7 @@
         return remote(slot, slot, pass_sem, (off,), sibling)
 
     def meta_copy(off):
-        return remote(meta_ref, meta_got.at[chip], meta_sem, (off,), same_core(off))
+        return remote(meta_send, meta_got.at[chip], meta_sem, (off,), same_core(off))
 
     def frames_of(b):
         return pl.ds(b * batch, batch)
@@ -228,6 +226,9 @@
     images.start()
     for a, b in offsets:
         pl.semaphore_signal(barrier, inc=1, device_id=peer(a, b), device_id_type=MESH)
+    meta_send[...] = jnp.zeros_like(meta_send)
+    meta_send[:priors, :particles] = priors_ref[...]
+    meta_send[priors : priors + 1, :particles] = defocus_ref[...]
     table = forward_ref[...].astype(BF16)
     swap = swap_ref[...]
     harmonics(ref_ref, cls_send, swap, table, place)
@@ -243,7 +244,7 @@
         for off in range(1, chips):
             part_copy(off, b).start()
     part_got[chip] = part_send[chip]
-    meta_got[chip] = meta_ref[...]
+    meta_got[chip] = meta_send[...]
     sums[...] = jnp.zeros_like(sums)
     norms[...] = jnp.zeros_like(norms)
     for off in range(1, chips):
@@ -254,9 +255,10 @@
 
     @pl.loop(0, chips)
     def _(src):
-        ctf_got[src] = ctf_rows(meta_got[src], priors, ctf_ref[...])
+        meta = meta_got[src].astype(F32).T[:particles].astype(jnp.int32)
+        ctf_got[src] = ctf_rows(meta, priors, ctf_ref[...])
         for b in range(BATCHES):
-            found = class_hits(meta_got[src, frames_of(b)], priors, classes)
+            found = class_hits(meta[b * batch : (b + 1) * batch], priors, classes)
             hits[src, b] = found.astype(BF16)
             hits_t[:, lanes_of(src, b)] = found.T.astype(BF16)
 
@@ -273,7 +275,7 @@
         for s in range(share):
             part = part_got[src, s, frames_of(b)].astype(F32)
             part = part * column(ctf, first_cycle[s] + chip_step * chip)
-            scaled[src, s, frames_of(b)] = part
+            scaled[src, s, frames_of(b)] = part.astype(BF16)
             table = cls_got[:, s].reshape(classes, width)
             picked = jnp.dot(hits[src, b], table, preferred_element_type=F32)
             picked = picked.reshape(priors, batch, width)
@@ -315,12 +317,12 @@
     other_half, own_half = ((1 - core) * half, core * half) if deliver else (0, 0)
 
     def slot_terms(src, b, s):
-        spectrum = spec_got[src, b].astype(F32)
+        spectrum = spec_got[src, b]
         wc, ws = spectrum[:, :, :harm], spectrum[:, :, harm:]
         part = scaled[src, s, frames_of(b)][None]
         pc, ps = part[:, :, :harm], part[:, :, harm:]
         both = jnp.concatenate([pc * wc + ps * ws, ps * wc - pc * ws], axis=2)
-        return both.reshape(slots, width).astype(BF16)
+        return both.reshape(slots, width)
 
     def add(src, b):
         chosen = hits_t[:, lanes_of(src, b)]
@@ -400,16 +402,23 @@
         sum_copy(a, b).wait()
     for a in range(1, doms):
         norm_copy(a).wait()
-    total_norm = norm_got[0, :, :cycles]
+
+
+def finish_body(cycles, sum_ref, norm_ref, out_ref, low, high):
+    doms, owners, run, owned, width = sum_ref.shape
+    harm = width // 2
+    held = owners * run
+    dom = lax.axis_index("dom")
+    norms = norm_ref[0, :, :cycles]
     for a in range(1, doms):
-        total_norm = total_norm + norm_got[a, :, :cycles]
+        norms = norms + norm_ref[a, :, :cycles]
     for c in range(owners):
         for one in range(run):
             cycle = c * run + one
-            result = sum_got[0, c, one].astype(F32)
+            result = sum_ref[0, c, one].astype(F32)
             for a in range(1, doms):
-                result = result + sum_got[a, c, one].astype(F32)
-            result = result / (column(total_norm, dom * held + cycle) + 1.0)
+                result = result + sum_ref[a, c, one].astype(F32)
+            result = result / (column(norms, dom * held + cycle) + 1.0)
             at = pl.ds(cycle, owned, stride=held)
             low[at, :] = result[:, :harm]
             high[at, :] = result[:, harm:]
@@ -431,11 +440,11 @@
     run = max(held // owners, 1)
     forward, inverse = (jnp.asarray(t) for t in angle_tables(angles))
     swap = jnp.asarray(swap_matrix(), BF16)
-    meta = jnp.concatenate(
-        [priors, defocus[:, None], jnp.zeros((particles, 127 - prior_count), jnp.int32)], axis=1
-    )
     if deliver:
-        shapes = [jax.ShapeDtypeStruct((owned * held, width), F32)]
+        shapes = [
+            jax.ShapeDtypeStruct((doms, owners, run, owned, width), BF16),
+            jax.ShapeDtypeStruct((doms, owned, 2 * cycles), F32),
+        ]
     else:
         shapes = [
             jax.ShapeDtypeStruct((share, classes, width), BF16),
@@ -451,7 +460,7 @@
     done = pl.pallas_call(
         functools.partial(body, doms, chips, prior_count, deliver),
         out_shape=shapes,
-        in_specs=[pl.BlockSpec(memory_space=pl.ANY)] + [VMEM] * 6,
+        in_specs=[pl.BlockSpec(memory_space=pl.ANY)] + [VMEM] * 7,
         out_specs=[VMEM] * len(shapes),
         scratch_shapes=[
             pltpu.VMEM(images.shape, BF16),
@@ -459,8 +468,9 @@
             pltpu.VMEM((chips, share, particles, width), BF16),
             pltpu.VMEM((chips, share, owned, width), BF16),
             pltpu.VMEM((owners, share, owned, width), BF16),
-            pltpu.VMEM((chips,) + meta.shape, jnp.int32),
-            pltpu.VMEM((chips, share, particles, width), F32),
+            pltpu.VMEM((16, 128), jnp.int32),
+            pltpu.VMEM((chips, 16, 128), jnp.int32),
+            pltpu.VMEM((chips, share, particles, width), BF16),
             pltpu.VMEM((chips, particles, cycles), F32),
             pltpu.VMEM((chips, BATCHES, rows, classes), BF16),
             pltpu.VMEM((classes, chips * BATCHES * rows), BF16),
@@ -476,11 +486,7 @@
             pltpu.VMEM((owned, 2 * cycles), F32),
             pltpu.VMEM((owned, 2 * cycles), F32),
             pltpu.VMEM(half, BF16),
-            pltpu.VMEM((doms, owners, run, owned, width), BF16),
             pltpu.VMEM((owned, 2 * cycles), F32),
-            pltpu.VMEM((doms, owned, 2 * cycles), F32),
-            pltpu.VMEM((owned * held, width // 2), F32),
-            pltpu.VMEM((owned * held, width // 2), F32),
             pltpu.SemaphoreType.DMA,
             pair_sem,
             pair_sem,
@@ -495,9 +501,17 @@
         compiler_params=pltpu.CompilerParams(
             collective_id=1, has_side_effects=True, vmem_limit_bytes=LIMIT
         ),
-    )(images, references, meta, ctf_table, swap, forward, inverse)
+    )(images, references, priors.T, defocus[None, :], ctf_table, swap, forward, inverse)
     if deliver:
-        return done[0].reshape(owned, held, width)
+        done = pl.pallas_call(
+            functools.partial(finish_body, cycles),
+            out_shape=jax.ShapeDtypeStruct((owned * held, width), F32),
+            in_specs=[VMEM] * 2,
+            out_specs=VMEM,
+            scratch_shapes=[pltpu.VMEM((owned * held, width // 2), F32)] * 2,
+            compiler_params=pltpu.CompilerParams(vmem_limit_bytes=LIMIT),
+        )(*done)
+        return done.reshape(owned, held, width)
     sums, norms = done
     me = lax.axis_index("cls")
     chip = me // CORES

time: 59.9 us -> 57.5 us (0.960)
  local copies, waits for them, and re-layouts: 3.09 us -> 0 us
  Pallas kernels: 55.8 us -> 57.2 us
  other arithmetic: 0.68 us -> 0 us
    unnamed x6 -> x0, local copies, waits for them, and re-layouts: 2.93 us -> none
    pallas_call x0 -> x1, Pallas kernels: none -> 1.97 us  [on_device(): pl.pallas_call(functools.partial(finish_body, cycles), out_shape=jax.Shap...]
    concatenate x1 -> x0, other arithmetic: 0.68 us -> none  [on_device(): jnp.concatenate([priors, defocus[:, None], jnp.zeros((particles, 127 - pr...]
where the time goes in v5:
time: 57.5 us; the launch traced here: 57.3 us
  Pallas kernels  57.2 us (99%)
    pallas_call x1, Pallas kernels, on_device(): pl.pallas_call(functools.partial(body, doms, chips, prior_count, deliver)...  55.3 us
    pallas_call x1, Pallas kernels, on_device(): pl.pallas_call(functools.partial(finish_body, cycles), out_shape=jax.Shap...  1.97 us

profile of v5, /device:TPU:0, one launch (start us, length us, event | category | flops | bytes accessed | tf_op | source)
XLA Modules:
  0.0 57.3 jit_solution(15865760648741622058)
XLA Ops:
  0.0 55.3 %shard_map.82 = (bf16[4,8,2,16,256]{4,3,2,1,0:T(8,128)(2,1)}, f32[4,16,128]{2,1,0:T(8,128)}) custom-call(bf16[32,64,256]{2,1,0:T(8,128)(2,1)} %img_ref.1, bf16[16,64,256]{2,1,0:T(8,128)(2,1)} %ref_ref.1, s32[8,32]{1,0:T(8,128)} %bitcast.3, s32[1,32]{1,0:T(1,128)} %bitcast.4, f32[64,64]{1,0:T(8,128)} %ctf_ref.1, bf16[256,256]{1,0:T(8,128)(2,1)} %constant.8.clone.swap_ref, ...), custom_call_target="tpu_custom_call" | custom-call | tf_op jit(solution)/shard_map/pallas_call | solution.py:460
  55.3 2.0 %shard_map.83 = f32[256,256]{1,0:T(8,128)} custom-call(bf16[4,8,2,16,256]{4,3,2,1,0:T(8,128)(2,1)} %get-tuple-element.7.sum_ref, f32[4,16,128]{2,1,0:T(8,128)} %get-tuple-element.8.norm_ref), custom_call_target="tpu_custom_call" | custom-call | tf_op jit(solution)/shard_map/pallas_call | solution.py:506

commit v6 on v5

--- a/solution.py
+++ b/solution.py
@@ -37,10 +37,10 @@
     return swap
 
 
-def harmonics(src, dst, swap, table, place):
-    frames, cycles, angles = src.shape
+def harmonics(src, dst, swap, table, place, frames):
+    cycles, angles = src.shape[1:]
     for first in range(0, cycles, TILE):
-        for frame in range(0, frames, TILE):
+        for frame in range(*frames, TILE):
             block = src[frame : frame + TILE, first : first + TILE, :]
             block = block.reshape(TILE * TILE, angles)
             block = jnp.dot(swap, block, preferred_element_type=F32).astype(BF16)
@@ -128,6 +128,7 @@
         norm_send,
         img_sem,
         cls_sem,
+        cross_sem,
         pass_sem,
         meta_sem,
         part_sem,
@@ -163,13 +164,18 @@
     chip_step = places[1, 0] - places[0, 0]
 
     barrier = pltpu.get_barrier_semaphore()
-    offsets = [(a, b) for a in range(doms if deliver else 1) for b in range(owners)][1:]
+    offsets = [(a, b) for a in range(doms) for b in range(owners)][1:]
 
     def peer(a, b):
         return (lax.rem(dom + a, doms), lax.rem(me + b, owners))
 
     def chip_at(off):
-        return lax.rem(chip + off + chips, chips)
+        number, bit = 0, 1
+        while bit < chips:
+            ours, flip = chip // bit % 2, off // bit % 2
+            number = number + bit * (ours + flip - 2 * ours * flip)
+            bit *= 2
+        return number
 
     def remote(src, dst, sem, at, device):
         return pltpu.make_async_remote_copy(
@@ -184,16 +190,32 @@
     def same_core(off):
         return (dom, chip_at(off) * CORES + core)
 
+    upper = dom % 2
+    partner = (dom + 1 - 2 * upper, me)
+    part_share = share // 2
+
+    def cycle_half(h):
+        return pl.ds((upper + h - 2 * upper * h) * part_share, part_share)
+
     def cls_copy(off):
-        return remote(cls_send.at[chip_at(off)], cls_got.at[me], cls_sem, (off,), same_core(off))
-
-    def pass_copy(off):
-        slot = cls_got.at[chip_at(-off) * CORES + core]
-        return remote(slot, slot, pass_sem, (off,), sibling)
-
-    def pass_got(off):
-        slot = cls_got.at[chip_at(-off) * CORES + 1 - core]
-        return remote(slot, slot, pass_sem, (off,), sibling)
+        src = cls_send.at[chip_at(off), cycle_half(0)]
+        return remote(src, cls_got.at[me, cycle_half(0)], cls_sem, (off,), same_core(off))
+
+    def cross_copy(off):
+        slot = cls_got.at[chip_at(off) * CORES + core, cycle_half(0)]
+        return remote(slot, slot, cross_sem, (off,), partner)
+
+    def cross_got(off):
+        slot = cls_got.at[chip_at(off) * CORES + core, cycle_half(1)]
+        return remote(slot, slot, cross_sem, (off,), partner)
+
+    def pass_copy(off, h):
+        slot = cls_got.at[chip_at(off) * CORES + core, cycle_half(h)]
+        return remote(slot, slot, pass_sem, (off, h), sibling)
+
+    def pass_got(off, h):
+        slot = cls_got.at[chip_at(off) * CORES + 1 - core, cycle_half(h)]
+        return remote(slot, slot, pass_sem, (off, h), sibling)
 
     def meta_copy(off):
         return remote(meta_send, meta_got.at[chip], meta_sem, (off,), same_core(off))
@@ -212,11 +234,11 @@
 
     def score_copy(off, b):
         return remote(
-            score_send.at[chip_at(-off), b],
+            score_send.at[chip_at(off), b],
             score_got.at[chip, b],
             score_sem,
             (off, b),
-            same_core(-off),
+            same_core(off),
         )
 
     def spec_copy(off, b):
@@ -231,22 +253,27 @@
     meta_send[priors : priors + 1, :particles] = defocus_ref[...]
     table = forward_ref[...].astype(BF16)
     swap = swap_ref[...]
-    harmonics(ref_ref, cls_send, swap, table, place)
+    harmonics(ref_ref, cls_send, swap, table, place, (0, owned))
     cls_got[me] = cls_send[chip]
     pl.semaphore_wait(barrier, len(offsets))
     for off in range(1, chips):
         meta_copy(off).start()
         cls_copy(off).start()
-    pass_copy(0).start()
+    for h in range(2):
+        pass_copy(0, h).start()
     images.wait()
-    harmonics(img_got, part_send, swap, table, place)
-    for b in range(BATCHES):
+    for b in range(BATCHES):
+        harmonics(img_got, part_send, swap, table, place, (b * batch, (b + 1) * batch))
         for off in range(1, chips):
             part_copy(off, b).start()
     part_got[chip] = part_send[chip]
     meta_got[chip] = meta_send[...]
     sums[...] = jnp.zeros_like(sums)
     norms[...] = jnp.zeros_like(norms)
+    for off in range(1, chips):
+        cls_copy(off).wait_recv()
+        cross_copy(off).start()
+        pass_copy(off, 0).start()
     for off in range(1, chips):
         meta_copy(off).wait()
 
@@ -263,11 +290,15 @@
             hits_t[:, lanes_of(src, b)] = found.T.astype(BF16)
 
     for off in range(1, chips):
-        cls_copy(off).wait()
-        pass_copy(off).start()
+        cross_got(off).wait_recv()
+        pass_copy(off, 1).start()
+    for off in range(1, chips):
+        cls_copy(off).wait_send()
+        cross_copy(off).wait_send()
     for off in range(chips):
-        pass_copy(off).wait_send()
-        pass_got(off).wait_recv()
+        for h in range(2):
+            pass_copy(off, h).wait_send()
+            pass_got(off, h).wait_recv()
 
     def score(src, b):
         ctf = ctf_got[src, frames_of(b)]
@@ -293,7 +324,7 @@
         @pl.loop(1, chips)
         def _(off):
             part_copy(off, b).wait_recv()
-            score(chip_at(-off), b)
+            score(chip_at(off), b)
             score_copy(off, b).start()
 
     for b in range(BATCHES):
@@ -342,7 +373,7 @@
         @pl.loop(1, chips)
         def _(off):
             spec_copy(off, b).wait_recv()
-            add(chip_at(-off), b)
+            add(chip_at(off), b)
 
     for b in range(BATCHES):
         for off in range(1, chips):
@@ -490,6 +521,7 @@
             pltpu.SemaphoreType.DMA,
             pair_sem,
             pair_sem,
+            pltpu.SemaphoreType.DMA((2, chips, 2)),
             pair_sem,
             batch_sem,
             batch_sem,

time: 57.5 us -> 55.1 us (0.958)
  Pallas kernels: 57.2 us -> 55 us
    pallas_call x1, Pallas kernels: 55.3 us -> 53 us  [on_device(): pl.pallas_call(functools.partial(body, doms, chips, prior_count, deliver)...]
where the time goes in v6:
time: 55.1 us; the launch traced here: 55 us
  Pallas kernels  55 us (100%)
    pallas_call x1, Pallas kernels, on_device(): pl.pallas_call(functools.partial(body, doms, chips, prior_count, deliver)...  53 us
    pallas_call x1, Pallas kernels, on_device(): pl.pallas_call(functools.partial(finish_body, cycles), out_shape=jax.Shap...  1.97 us

profile of v6, /device:TPU:0, one launch (start us, length us, event | category | flops | bytes accessed | tf_op | source)
XLA Modules:
  0.0 55.0 jit_solution(12487605598823828079)
XLA Ops:
  0.0 53.0 %shard_map.82 = (bf16[4,8,2,16,256]{4,3,2,1,0:T(8,128)(2,1)}, f32[4,16,128]{2,1,0:T(8,128)}) custom-call(bf16[32,64,256]{2,1,0:T(8,128)(2,1)} %img_ref.1, bf16[16,64,256]{2,1,0:T(8,128)(2,1)} %ref_ref.1, s32[8,32]{1,0:T(8,128)} %bitcast.3, s32[1,32]{1,0:T(1,128)} %bitcast.4, f32[64,64]{1,0:T(8,128)} %ctf_ref.1, bf16[256,256]{1,0:T(8,128)(2,1)} %constant.8.clone.swap_ref, ...), custom_call_target="tpu_custom_call" | custom-call | tf_op jit(solution)/shard_map/pallas_call | solution.py:491
  53.0 2.0 %shard_map.83 = f32[256,256]{1,0:T(8,128)} custom-call(bf16[4,8,2,16,256]{4,3,2,1,0:T(8,128)(2,1)} %get-tuple-element.7.sum_ref, f32[4,16,128]{2,1,0:T(8,128)} %get-tuple-element.8.norm_ref), custom_call_target="tpu_custom_call" | custom-call | tf_op jit(solution)/shard_map/pallas_call | solution.py:538

commit v7 on v6

--- a/solution.py
+++ b/solution.py
@@ -389,12 +389,20 @@
 
     mine = pl.multiple_of(me * owned, owned)
     other = pl.multiple_of(sibling[1] * owned, owned)
-    half_send[...] = sums[...].astype(BF16)
+    order = sorted(range(doms), key=lambda a: (a == 0, abs(a - doms // 2)))
+
+    def half_copy(a):
+        at = pl.ds(peer(a, 0)[0] * run, run)
+        return remote(half_send.at[at], half_got.at[at], half_sem, (a,), sibling)
+
+    for a in order:
+        at = pl.ds(peer(a, 0)[0] * run, run)
+        half_send[at] = sums[at].astype(BF16)
+        half_copy(a).start()
     half_norm[...] = norms[pl.ds(other, owned), :]
-    sum_half = remote(half_send, half_got, half_sem, (0,), sibling)
-    norm_half = remote(half_norm, half_norm_got, half_sem, (1,), sibling)
-    sum_half.start()
+    norm_half = remote(half_norm, half_norm_got, half_sem, (doms,), sibling)
     norm_half.start()
+
     def sum_copy(a, b):
         to = peer(a, b)
         start = pl.multiple_of(to[1] * owned, owned)
@@ -404,8 +412,7 @@
     def norm_copy(a):
         return remote(norm_send, norm_got.at[dom], norm_sem, (a,), peer(a, 0))
 
-    waited = False
-    for a in sorted(range(doms), key=lambda a: (a == 0, abs(a - doms // 2))):
+    for a in order:
         first = peer(a, 0)[0] * run
         own = []
         for one in range(run):
@@ -414,19 +421,18 @@
                     at = pl.ds((src * BATCHES + b) * slots, slots)
                     terms[one, at, :] = slot_terms(src, b, own_half + first + one)
             own.append(jnp.dot(hits_t[...], terms[one], preferred_element_type=F32))
-        if not waited:
-            sum_half.wait()
-            norm_half.wait()
-            norm_send[...] = norms[pl.ds(mine, owned), :] + half_norm_got[...]
-            waited = True
+        half_copy(a).wait()
         for one in range(run):
             both = own[one] + half_got[first + one].astype(F32)
             sum_send[first + one] = both.astype(BF16)
         for b in range(owners):
             if (a, b) in offsets:
                 sum_copy(a, b).start()
-        if a:
-            norm_copy(a).start()
+        if a == order[0]:
+            norm_half.wait()
+            norm_send[...] = norms[pl.ds(mine, owned), :] + half_norm_got[...]
+            for to in range(1, doms):
+                norm_copy(to).start()
     sum_got[dom, me] = sum_send[pl.ds(dom * run, run), pl.ds(mine, owned), :]
     norm_got[dom] = norm_send[...]
     for a, b in offsets:
@@ -526,7 +532,7 @@
             batch_sem,
             batch_sem,
             batch_sem,
-            pltpu.SemaphoreType.DMA((2, 2)),
+            pltpu.SemaphoreType.DMA((2, doms + 1)),
             pltpu.SemaphoreType.DMA((2, doms, owners)),
             pltpu.SemaphoreType.DMA((2, doms)),
         ],

time: 55.1 us -> 55.1 us (level)
  no operation moved by 1% of the time
where the time goes in v7:
time: 55.1 us; the launch traced here: 54.9 us
  Pallas kernels  54.9 us (100%)
    pallas_call x1, Pallas kernels, on_device(): pl.pallas_call(functools.partial(body, doms, chips, prior_count, deliver)...  53 us
    pallas_call x1, Pallas kernels, on_device(): pl.pallas_call(functools.partial(finish_body, cycles), out_shape=jax.Shap...  1.97 us

profile of v7, /device:TPU:0, one launch (start us, length us, event | category | flops | bytes accessed | tf_op | source)
XLA Modules:
  0.0 54.9 jit_solution(4841386028725382078)
XLA Ops:
  0.0 53.0 %shard_map.82 = (bf16[4,8,2,16,256]{4,3,2,1,0:T(8,128)(2,1)}, f32[4,16,128]{2,1,0:T(8,128)}) custom-call(bf16[32,64,256]{2,1,0:T(8,128)(2,1)} %img_ref.1, bf16[16,64,256]{2,1,0:T(8,128)(2,1)} %ref_ref.1, s32[8,32]{1,0:T(8,128)} %bitcast.3, s32[1,32]{1,0:T(1,128)} %bitcast.4, f32[64,64]{1,0:T(8,128)} %ctf_ref.1, bf16[256,256]{1,0:T(8,128)(2,1)} %constant.8.clone.swap_ref, ...), custom_call_target="tpu_custom_call" | custom-call | tf_op jit(solution)/shard_map/pallas_call | solution.py:497
  53.0 2.0 %shard_map.83 = f32[256,256]{1,0:T(8,128)} custom-call(bf16[4,8,2,16,256]{4,3,2,1,0:T(8,128)(2,1)} %get-tuple-element.7.sum_ref, f32[4,16,128]{2,1,0:T(8,128)} %get-tuple-element.8.norm_ref), custom_call_target="tpu_custom_call" | custom-call | tf_op jit(solution)/shard_map/pallas_call | solution.py:544

commit v8 on v7

--- a/solution.py
+++ b/solution.py
@@ -111,6 +111,7 @@
         meta_got,
         scaled,
         ctf_got,
+        ctf_wide,
         hits,
         hits_t,
         terms,
@@ -283,7 +284,11 @@
     @pl.loop(0, chips)
     def _(src):
         meta = meta_got[src].astype(F32).T[:particles].astype(jnp.int32)
-        ctf_got[src] = ctf_rows(meta, priors, ctf_ref[...])
+        ctf = ctf_rows(meta, priors, ctf_ref[...])
+        ctf_got[src] = ctf
+        for s in range(share):
+            one = column(ctf, first_cycle[s] + chip_step * chip)
+            ctf_wide[src, s] = jnp.broadcast_to(one, (particles, harm))
         for b in range(BATCHES):
             found = class_hits(meta[b * batch : (b + 1) * batch], priors, classes)
             hits[src, b] = found.astype(BF16)
@@ -301,11 +306,11 @@
             pass_got(off, h).wait_recv()
 
     def score(src, b):
-        ctf = ctf_got[src, frames_of(b)]
         real, imag = 0.0, 0.0
         for s in range(share):
+            wide = ctf_wide[src, s, frames_of(b)]
             part = part_got[src, s, frames_of(b)].astype(F32)
-            part = part * column(ctf, first_cycle[s] + chip_step * chip)
+            part = part * jnp.concatenate([wide, wide], axis=1)
             scaled[src, s, frames_of(b)] = part.astype(BF16)
             table = cls_got[:, s].reshape(classes, width)
             picked = jnp.dot(hits[src, b], table, preferred_element_type=F32)
@@ -509,6 +514,7 @@
             pltpu.VMEM((chips, 16, 128), jnp.int32),
             pltpu.VMEM((chips, share, particles, width), BF16),
             pltpu.VMEM((chips, particles, cycles), F32),
+            pltpu.VMEM((chips, share, particles, width // 2), F32),
             pltpu.VMEM((chips, BATCHES, rows, classes), BF16),
             pltpu.VMEM((classes, chips * BATCHES * rows), BF16),
             pltpu.VMEM((run, chips * BATCHES * rows, width), BF16),

time: 55.1 us -> 55.1 us (level)
  no operation moved by 1% of the time
where the time goes in v8:
time: 55.1 us; the launch traced here: 54.9 us
  Pallas kernels  54.9 us (100%)
    pallas_call x1, Pallas kernels, on_device(): pl.pallas_call(functools.partial(body, doms, chips, prior_count, deliver)...  53 us
    pallas_call x1, Pallas kernels, on_device(): pl.pallas_call(functools.partial(finish_body, cycles), out_shape=jax.Shap...  1.97 us

profile of v8, /device:TPU:0, one launch (start us, length us, event | category | flops | bytes accessed | tf_op | source)
XLA Modules:
  0.0 54.9 jit_solution(3084250902734475709)
XLA Ops:
  0.0 53.0 %shard_map.82 = (bf16[4,8,2,16,256]{4,3,2,1,0:T(8,128)(2,1)}, f32[4,16,128]{2,1,0:T(8,128)}) custom-call(bf16[32,64,256]{2,1,0:T(8,128)(2,1)} %img_ref.1, bf16[16,64,256]{2,1,0:T(8,128)(2,1)} %ref_ref.1, s32[8,32]{1,0:T(8,128)} %bitcast.3, s32[1,32]{1,0:T(1,128)} %bitcast.4, f32[64,64]{1,0:T(8,128)} %ctf_ref.1, bf16[256,256]{1,0:T(8,128)(2,1)} %constant.8.clone.swap_ref, ...), custom_call_target="tpu_custom_call" | custom-call | tf_op jit(solution)/shard_map/pallas_call | solution.py:502
  53.0 2.0 %shard_map.83 = f32[256,256]{1,0:T(8,128)} custom-call(bf16[4,8,2,16,256]{4,3,2,1,0:T(8,128)(2,1)} %get-tuple-element.7.sum_ref, f32[4,16,128]{2,1,0:T(8,128)} %get-tuple-element.8.norm_ref), custom_call_target="tpu_custom_call" | custom-call | tf_op jit(solution)/shard_map/pallas_call | solution.py:550
